TPU v7x, 256 devices: a whole 4x4x8 slice. The times are simulated.
256 devices in a mesh: tm: 16 (over y_hi, z), height: 16 (over y_lo, x, core).
Axes of the slice: x: 4, y: 4 (y_hi: 2, y_lo: 2; y = y_hi * 2 + y_lo), z: 8, core: 2. Of those that a mesh axis runs over, the one named last changes fastest.
Arguments:
- saved: bfloat16 [2, 4, 32, 128, 16, 1536], P(None, None, 'tm', 'height'), may hold values from -600 to 600
- gains: float32 [2, 2, 12, 128], replicated, may hold values from 0.5 to 6
Outputs:
- grads: bfloat16 [2, 3, 32, 128, 16, 1536], P(None, None, 'tm', 'height')
- gain_grads: float32 [2, 2, 12, 128], replicated
All inputs are finite; a program needn't handle non-finite values.
Results may differ from a plain program's by a relative error of at most 0.0039.
The roundings to bfloat16 on the way count: a program that leaves them out, or rounds other values in their place, can miss the bound.
Values may be sent and summed in bfloat16 or wider, within the bound.
A program may use at most 128 MiB of HBM per device.

v0:
```python
import jax
import jax.numpy as jnp
from jax import lax
from jax.sharding import PartitionSpec as P

HEADS = 12
HD = 128
WT = 2
WH = 8
WW = 16


EPSILON = 1e-06


def from_behind(block, axis, distance):
    devices = range(lax.axis_size(axis))
    route = [((i - distance) % len(devices), i) for i in devices]
    return lax.ppermute(block, axis, route)


def windows(array):
    frames, rows, cols, feats = array.shape
    blocked = array.reshape(frames // WT, WT, rows // WH, WH, cols // WW, WW, HEADS, HD)
    blocked = blocked.transpose(0, 2, 4, 6, 1, 3, 5, 7)
    return blocked.reshape(-1, HEADS, WT * WH * WW, HD)


def unwindows(blocked, layout):
    frames, rows, cols, feats = layout
    grid = blocked.reshape(frames // WT, rows // WH, cols // WW, HEADS, WT, WH, WW, HD)
    return grid.transpose(0, 4, 1, 5, 2, 6, 3, 7).reshape(frames, rows, cols, feats)


def raw_grad(norm_grad, unit, inverse, gain):
    scaled = norm_grad * gain[:, None, :]
    return (inverse * (scaled - unit * jnp.mean(scaled * unit, -1, keepdims=True))).astype(
        jnp.bfloat16
    )


def window_grad(q_raw, k_raw, values_in, out_grad, gain_q, gain_k):
    scale = HD ** (-0.5)
    q_full = q_raw.astype(jnp.float32)
    k_full = k_raw.astype(jnp.float32)
    inv_q = lax.rsqrt(jnp.mean(q_full * q_full, -1, keepdims=True) + EPSILON)
    inv_k = lax.rsqrt(jnp.mean(k_full * k_full, -1, keepdims=True) + EPSILON)
    unit_q = q_full * inv_q
    unit_k = k_full * inv_k
    q_norm = (unit_q * gain_q[:, None, :]).astype(jnp.bfloat16)
    k_norm = (unit_k * gain_k[:, None, :]).astype(jnp.bfloat16)
    scores = (
        jnp.einsum("nhqd,nhkd->nhqk", q_norm, k_norm, preferred_element_type=jnp.float32) * scale
    )
    attn_probs = jnp.exp(scores - jnp.max(scores, -1, keepdims=True))
    attn_probs = attn_probs / jnp.sum(attn_probs, -1, keepdims=True)
    probs_low = attn_probs.astype(jnp.bfloat16)
    prob_grad = jnp.einsum(
        "nhqd,nhkd->nhqk", out_grad, values_in, preferred_element_type=jnp.float32
    )
    score_grad = attn_probs * (prob_grad - jnp.sum(attn_probs * prob_grad, -1, keepdims=True))
    score_grad = score_grad.astype(jnp.bfloat16)
    value_grad = jnp.einsum(
        "nhqk,nhqd->nhkd", probs_low, out_grad, preferred_element_type=jnp.float32
    ).astype(jnp.bfloat16)
    qn_grad = (
        jnp.einsum("nhqk,nhkd->nhqd", score_grad, k_norm, preferred_element_type=jnp.float32)
        * scale
    )
    kn_grad = (
        jnp.einsum("nhqk,nhqd->nhkd", score_grad, q_norm, preferred_element_type=jnp.float32)
        * scale
    )
    gain_q_grad = jnp.sum(qn_grad * unit_q, axis=(0, 2))
    gain_k_grad = jnp.sum(kn_grad * unit_k, axis=(0, 2))
    return (
        raw_grad(qn_grad, unit_q, inv_q, gain_q),
        raw_grad(kn_grad, unit_k, inv_k, gain_k),
        value_grad,
        gain_q_grad,
        gain_k_grad,
    )


def block_grad(stacked, gain_pair):
    layout = stacked.shape[1:]
    pieces = [windows(stacked[index]) for index in range(4)]
    results = window_grad(pieces[0], pieces[1], pieces[2], pieces[3], gain_pair[0], gain_pair[1])
    grads_block = jnp.stack([unwindows(results[index], layout) for index in range(3)])
    gains_block = jnp.stack([results[3], results[4]])
    return (grads_block, gains_block)


def frames_in(stacked):
    half_t = WT // 2
    moved = from_behind(stacked[:, :half_t], "tm", -1)
    return jnp.concatenate([stacked[:, half_t:], moved], axis=1)


def rows_in(stacked):
    half_h = WH // 2
    moved = from_behind(stacked[:, :, :half_h], "height", -1)
    return jnp.concatenate([stacked[:, :, half_h:], moved], axis=2)


def frames_out(stacked):
    keep_t = WT - WT // 2
    moved = from_behind(stacked[:, keep_t:], "tm", 1)
    return jnp.concatenate([moved, stacked[:, :keep_t]], axis=1)


def rows_out(stacked):
    keep_h = WH - WH // 2
    moved = from_behind(stacked[:, :, keep_h:], "height", 1)
    return jnp.concatenate([moved, stacked[:, :, :keep_h]], axis=2)


def shards(saved, gains):
    shifted = saved[1]
    shifted = rows_in(frames_in(shifted))
    shifted = jnp.roll(shifted, -(WW // 2), axis=3)
    grads_one, gains_one = block_grad(shifted, gains[1])
    grads_one = jnp.roll(grads_one, WW // 2, axis=3)
    grads_one = rows_out(frames_out(grads_one))
    grads_zero, gains_zero = block_grad(saved[0], gains[0])
    gains_one, gains_zero = lax.psum((gains_one, gains_zero), ("tm", "height"))
    return (jnp.stack([grads_zero, grads_one]), jnp.stack([gains_zero, gains_one]))


def solution(mesh):
    return jax.shard_map(
        shards,
        mesh=mesh,
        in_specs=(P(None, None, "tm", "height", None, None), P()),
        out_specs=(P(None, None, "tm", "height", None, None), P()),
        check_vma=False,
    )
```

profile of v0, /device:TPU:1, one launch (start us, length us, event | category | flops | bytes accessed | tf_op | source)
XLA Modules:
  0.0 268.1 jit_solution(12677334140129948257)
XLA Ops:
  4.6 9.0 %collective-permute-start = (bf16[4,1,8,16,1536]{4,3,2,1,0:T(8,128)(2,1)}, bf16[4,1,8,16,1536]{4,3,2,1,0:T(8,128)(2,1)}, u32[]{:S(2)}, u32[]{:S(2)}) collective-permute-start(bf16[4,1,8,16,1536]{4,3,2,1,0:T(8,128)(2,1)} %get-tuple-element.27), channel_id=1, source_target_pairs={{16,0},{32,16},{48,32},{64,48},{80,64},{96,80},{112,96},{128,112},... | collective-permute-start | bytes 4718600 | tf_op jit(solution)/shard_map/ppermute | solution.py:19
  34.4 3.2 %fusion.41 = (f32[12,256]{1,0:T(8,128)S(1)}, f32[12,256,256]{1,2,0:T(8,128)}) fusion(f32[12,256,128]{2,1,0:T(8,128)S(1)} %bitcast.124, f32[12,128]{1,0:T(8,128)S(1)} %get-tuple-element.51, f32[12,256]{1,0:T(8,128)S(1)} %copy.43, f32[12,256,128]{2,1,0:T(8,128)S(1)} %bitcast.128, f32[12,128]{1,0:T(8,128)S(1)} %get-tuple-element.50, f32[12,256]{1,0:T(8,128)S(1)} %copy.47), kind=kOutput, calls=%fused_computation.102 | convolution fusion | flops 206045440 | bytes 6340608 | tf_op jit(solution)/shard_map/sub | solution.py:55
  37.6 2.6 fusion.18
  41.8 2.4 stack_reshape.20
  44.2 2.8 %collective-permute-done = bf16[4,1,8,16,1536]{4,3,2,1,0:T(8,128)(2,1)} collective-permute-done((bf16[4,1,8,16,1536]{4,3,2,1,0:T(8,128)(2,1)}, bf16[4,1,8,16,1536]{4,3,2,1,0:T(8,128)(2,1)}, u32[]{:S(2)}, u32[]{:S(2)}) %collective-permute-start) | collective-permute-done | bytes 1572896 | tf_op jit(solution)/shard_map/ppermute | solution.py:19
  53.3 16.8 %collective-permute-done.1 = bf16[4,2,4,16,1536]{4,3,2,1,0:T(8,128)(2,1)S(1)} collective-permute-done((bf16[4,2,4,16,1536]{4,3,2,1,0:T(8,128)(2,1)S(1)}, bf16[4,2,4,16,1536]{4,3,2,1,0:T(8,128)(2,1)S(1)}, u32[]{:S(2)}, u32[]{:S(2)}) %collective-permute-start.1) | collective-permute-done | bytes 1572896 | tf_op jit(solution)/shard_map/ppermute | solution.py:19
  75.2 2.7 mul.366
  80.2 2.7 %reshape.409 = f32[1,2,1,8,1,16,12,128]{7,6,5,3,1,4,2,0:T(8,128)} reshape(f32[1,2,8,16,1536]{4,3,2,1,0:T(8,128)} %get-tuple-element.20) | data formatting | bytes 3145728 | tf_op jit(solution)/shard_map/convert_element_type | solution.py:45
  82.8 3.2 %copy.58 = f32[1,1,1,12,2,8,16,128]{7,6,5,4,3,2,1,0:T(8,128)} copy(f32[1,1,1,12,2,8,16,128]{7,3,6,5,4,2,1,0:T(8,128)} %bitcast.142) | data formatting | bytes 3145728 | tf_op jit(solution)/shard_map/convert_element_type | solution.py:45
  93.1 2.4 copy.61
  95.5 2.7 reshape.408
  98.2 3.3 %copy.56 = f32[1,1,1,12,2,8,16,128]{7,6,5,4,3,2,1,0:T(8,128)} copy(f32[1,1,1,12,2,8,16,128]{7,3,6,5,4,2,1,0:T(8,128)} %bitcast.143) | data formatting | bytes 3145728 | tf_op jit(solution)/shard_map/convert_element_type | solution.py:44
  101.5 2.7 mul.359
  106.5 5.0 %fusion.40 = (f32[12,256]{1,0:T(8,128)S(1)}, f32[12,256,256]{1,2,0:T(8,128)}) fusion(f32[12,256,128]{2,1,0:T(8,128)} %bitcast.136, f32[12,128]{1,0:T(8,128)S(1)} %get-tuple-element.49, f32[12,256]{1,0:T(8,128)S(1)} %copy.55, f32[12,256,128]{2,1,0:T(8,128)} %bitcast.132, f32[12,128]{1,0:T(8,128)S(1)} %get-tuple-element.48, f32[12,256]{1,0:T(8,128)S(1)} %copy.59), kind=kOutput, calls=%fused_computation.101 | convolution fusion | flops 206045440 | bytes 6340608 | tf_op jit(solution)/shard_map/sub | solution.py:55
  111.5 2.6 fusion.21
  118.1 3.1 %multiply_reduce_fusion = (f32[12,256]{1,0:T(8,128)S(1)}, f32[12,256,256]{1,2,0:T(8,128)S(1)}) fusion(f32[12,256,256]{1,2,0:T(8,128)} %get-tuple-element.37, f32[12,256]{1,0:T(8,128)S(1)} %get-tuple-element.36, bf16[12,256,128]{2,1,0:T(8,128)(2,1)} %bitcast.163, bf16[12,256,128]{2,1,0:T(8,128)(2,1)} %bitcast.161), kind=kOutput, calls=%fused_computation.10 | convolution fusion | flops 203682816 | bytes 7888896 | tf_op jit(solution)/shard_map/nhqd,nhkd->nhqk/dot_general | solution.py:58
  123.3 3.2 %multiply_reduce_fusion.4 = (f32[12,128]{1,0:T(8,128)}, f32[12,256]{1,0:T(8,128)S(1)}, f32[12,256,128]{2,1,0:T(8,128)}) fusion(f32[12,256,128]{2,1,0:T(8,128)S(1)} %bitcast.134, f32[12,256]{1,0:T(8,128)S(1)} %copy.59, f32[12,128]{1,0:T(8,128)S(1)} %get-tuple-element.52, bf16[12,256,256]{1,2,0:T(8,128)(2,1)S(1)} %multiply_convert_fusion, ...), kind=kOutput, calls=%fused_computation.29 | convolution fusion | flops 205254144 | bytes 6346752 | tf_op jit(solution)/shard_map/nhqk,nhqd->nhkd/dot_general | solution.py:71
  126.5 3.5 %multiply_reduce_fusion.5 = (f32[12,128]{1,0:T(8,128)}, f32[12,256]{1,0:T(8,128)S(1)}, f32[12,256,128]{2,1,0:T(8,128)S(1)}) fusion(f32[12,256,128]{2,1,0:T(8,128)S(1)} %bitcast.138, f32[12,256]{1,0:T(8,128)S(1)} %copy.55, f32[12,128]{1,0:T(8,128)S(1)} %get-tuple-element.53, bf16[12,256,256]{1,2,0:T(8,128)(2,1)S(1)} %multiply_convert_fusion, ...), kind=kOutput, calls=%fused_computation.30 | convolution fusion | flops 205254144 | bytes 6346752 | tf_op jit(solution)/shard_map/nhqk,nhkd->nhqd/dot_general | solution.py:67
  138.9 2.4 stack_reshape.22
  145.9 3.5 %multiply_reduce_fusion.7 = (f32[12,128]{1,0:T(8,128)S(1)}, f32[12,256]{1,0:T(8,128)}, f32[12,256,128]{2,1,0:T(8,128)}) fusion(f32[12,256,128]{2,1,0:T(8,128)S(1)} %bitcast.125, f32[12,256]{1,0:T(8,128)S(1)} %copy.43, f32[12,128]{1,0:T(8,128)S(1)} %get-tuple-element.55, bf16[12,256,256]{1,2,0:T(8,128)(2,1)S(1)} %copy-done.2, ...), kind=kOutput, calls=%fused_computation.32 | convolution fusion | flops 205254144 | bytes 6346752 | tf_op jit(solution)/shard_map/nhqk,nhkd->nhqd/dot_general | solution.py:67
  150.0 2.7 %multiply_reduce_fusion.6 = (f32[12,128]{1,0:T(8,128)S(1)}, f32[12,256]{1,0:T(8,128)S(1)}, f32[12,256,128]{2,1,0:T(8,128)S(1)}) fusion(f32[12,256,128]{2,1,0:T(8,128)S(1)} %bitcast.130, f32[12,256]{1,0:T(8,128)S(1)} %copy.47, f32[12,128]{1,0:T(8,128)S(1)} %get-tuple-element.54, bf16[12,256,256]{1,2,0:T(8,128)(2,1)S(1)} %copy-done.2, ...), kind=kOutput, calls=%fused_computation.31 | convolution fusion | flops 205254144 | bytes 6346752 | tf_op jit(solution)/shard_map/nhqk,nhqd->nhkd/dot_general | solution.py:71
  158.3 18.5 %collective-permute-done.2 = bf16[3,1,8,16,1536]{4,3,2,1,0:T(8,128)(2,1)} collective-permute-done((bf16[3,1,8,16,1536]{4,3,2,1,0:T(8,128)(2,1)}, bf16[3,1,8,16,1536]{4,3,2,1,0:T(8,128)(2,1)}, u32[]{:S(2)}, u32[]{:S(2)}) %collective-permute-start.2) | collective-permute-done | bytes 1179680 | tf_op jit(solution)/shard_map/ppermute | solution.py:19
  185.9 76.8 %all-reduce = (f32[1,2,12,128]{3,1,2,0:T(2,128)}, f32[1,2,12,128]{3,1,2,0:T(2,128)}) all-reduce(f32[1,2,12,128]{3,1,2,0:T(2,128)} %maximum_bitcast_fusion.3, f32[1,2,12,128]{3,1,2,0:T(2,128)S(1)} %maximum_bitcast_fusion.2), channel_id=1, replica_groups=mesh['tm'=16,'height'=16] {'tm','height'}, use_global_device_ids=true, to_apply=%region_19.20 | all-reduce | flops 6144 | bytes 49152 | tf_op jit(solution)/shard_map/psum | solution.py:126
  265.5 2.6 pad_maximum_fusion
  (128 shorter events, 86.6 us)
Async XLA Ops:
  2.7 10.9 %copy-start.8 = (bf16[2,4,2,8,16,1536]{5,4,3,2,1,0:T(8,128)(2,1)S(1)}, bf16[2,4,2,8,16,1536]{5,4,3,2,1,0:T(8,128)(2,1)}, u32[]{:S(2)}) copy-start(bf16[2,4,2,8,16,1536]{5,4,3,2,1,0:T(8,128)(2,1)} %param.2) | copy-start | bytes 18874372
  4.6 42.4 %collective-permute-start = (bf16[4,1,8,16,1536]{4,3,2,1,0:T(8,128)(2,1)}, bf16[4,1,8,16,1536]{4,3,2,1,0:T(8,128)(2,1)}, u32[]{:S(2)}, u32[]{:S(2)}) collective-permute-start(bf16[4,1,8,16,1536]{4,3,2,1,0:T(8,128)(2,1)} %get-tuple-element.27), channel_id=1, source_target_pairs={{16,0},{32,16},{48,32},{64,48},{80,64},{96,80},{112,96},{128,112},... | collective-permute-start | bytes 4718600 | tf_op jit(solution)/shard_map/ppermute | solution.py:19
  25.2 1.6 copy-start.11
  28.4 2.2 copy-start.10
  32.3 2.1 copy-start.21
  44.2 100.8 %copy-start.16 = (f32[12,128]{1,0:T(8,128)}, f32[12,128]{1,0:T(8,128)S(1)}, u32[]{:S(2)}) copy-start(f32[12,128]{1,0:T(8,128)S(1)} %get-tuple-element.55) | copy-start | bytes 18436
  47.0 3.9 %copy-start.3 = (f32[12,256,256]{1,2,0:T(8,128)S(1)}, f32[12,256,256]{1,2,0:T(8,128)}, u32[]{:S(2)}) copy-start(f32[12,256,256]{1,2,0:T(8,128)} %get-tuple-element.43) | copy-start | bytes 9437188
  47.0 3.9 %copy-start.14 = (bf16[1,1,1,12,2,8,16,128]{7,6,5,4,3,2,1,0:T(8,128)(2,1)S(1)}, bf16[1,1,1,12,2,8,16,128]{7,6,5,4,3,2,1,0:T(8,128)(2,1)}, u32[]{:S(2)}) copy-start(bf16[1,1,1,12,2,8,16,128]{7,6,5,4,3,2,1,0:T(8,128)(2,1)} %copy.50) | copy-start | bytes 2359300
  47.0 3.9 %copy-start.15 = (bf16[1,1,1,12,2,8,16,128]{7,6,5,4,3,2,1,0:T(8,128)(2,1)S(1)}, bf16[1,1,1,12,2,8,16,128]{7,6,5,4,3,2,1,0:T(8,128)(2,1)}, u32[]{:S(2)}) copy-start(bf16[1,1,1,12,2,8,16,128]{7,6,5,4,3,2,1,0:T(8,128)(2,1)} %copy.49) | copy-start | bytes 2359300
  49.3 20.8 %collective-permute-start.1 = (bf16[4,2,4,16,1536]{4,3,2,1,0:T(8,128)(2,1)S(1)}, bf16[4,2,4,16,1536]{4,3,2,1,0:T(8,128)(2,1)S(1)}, u32[]{:S(2)}, u32[]{:S(2)}) collective-permute-start(bf16[4,2,4,16,1536]{4,3,2,1,0:T(8,128)(2,1)S(1)} %get-tuple-element.25), channel_id=1, source_target_pairs={{1,0},{2,1},{3,2},{4,3},{5,4},{6,5},{7,6},{8,7},{9,8},{10,9},{11,1... | collective-permute-start | bytes 4718600 | tf_op jit(solution)/shard_map/ppermute | solution.py:19
  118.1 3.3 %copy-start.4 = (f32[12,256,256]{1,2,0:T(8,128)S(1)}, f32[12,256,256]{1,2,0:T(8,128)}, u32[]{:S(2)}) copy-start(f32[12,256,256]{1,2,0:T(8,128)} %get-tuple-element.37) | copy-start | bytes 9437188
  121.4 1.9 copy-start.1
  141.3 1.6 copy-start.12
  143.3 1.8 copy-start.7
  143.3 2.6 copy-start.2
  145.1 31.7 %collective-permute-start.2 = (bf16[3,1,8,16,1536]{4,3,2,1,0:T(8,128)(2,1)}, bf16[3,1,8,16,1536]{4,3,2,1,0:T(8,128)(2,1)}, u32[]{:S(2)}, u32[]{:S(2)}) collective-permute-start(bf16[3,1,8,16,1536]{4,3,2,1,0:T(8,128)(2,1)} %fusion.24), channel_id=1, source_target_pairs={{240,0},{0,16},{16,32},{32,48},{48,64},{64,80},{80,96},{96,112},{1... | collective-permute-start | bytes 3538952 | tf_op jit(solution)/shard_map/ppermute | solution.py:19
  154.3 22.4 %copy-start.6 = (bf16[3,2,8,8,1536]{4,3,2,1,0:T(8,128)(2,1)S(1)}, bf16[3,2,8,8,1536]{4,3,2,1,0:T(8,128)(2,1)}, u32[]{:S(2)}) copy-start(bf16[3,2,8,8,1536]{4,3,2,1,0:T(8,128)(2,1)} %copy-done.5) | copy-start | bytes 3538948
  178.5 1.8 copy-start.9
  178.5 1.8 copy-start.17
  179.7 84.3 %collective-permute-start.3 = (bf16[3,2,4,16,1536]{4,3,2,1,0:T(8,128)(2,1)}, bf16[3,2,4,16,1536]{4,3,2,1,0:T(8,128)(2,1)}, u32[]{:S(2)}, u32[]{:S(2)}) collective-permute-start(bf16[3,2,4,16,1536]{4,3,2,1,0:T(8,128)(2,1)} %get-tuple-element.28), channel_id=1, source_target_pairs={{15,0},{0,1},{1,2},{2,3},{3,4},{4,5},{5,6},{6,7},{7,8},{8,9},{9,10... | collective-permute-start | bytes 3538952 | tf_op jit(solution)/shard_map/ppermute | solution.py:19
  181.3 2.0 copy-start.22
  181.4 2.0 copy-start.23
  183.3 1.9 copy-start.19
  183.4 1.9 copy-start.20
  (4 other events, 5.7 us)
where the time goes:
time: 269 us; the launch traced here: 268 us
  blocking collectives  76.8 us (29%)
  local copies, waits for them, and re-layouts  75 us (28%)
  waiting for transfers between devices  38.1 us (14%)
  other arithmetic  36.1 us (13%)
  matrix products  30.1 us (11%)
  starting transfers between devices  10.9 us (4%)
    psum x1, blocking collectives, shards(): gains_one, gains_zero = lax.psum((gains_one, gains_zero), ('tm', 'height'))  76.8 us
    ppermute x4, waiting for transfers between devices, from_behind(): return lax.ppermute(block, axis, route)  38.1 us
    another operation x7, local copies, waits for them, and re-layouts, block_grad(): jnp.stack([unwindows(results[index], layout) for index in range(3)])  13.4 us
    ppermute x4, starting transfers between devices, from_behind(): return lax.ppermute(block, axis, route)  10.9 us
    convert_element_type x4, local copies, waits for them, and re-layouts, window_grad(): k_full = k_raw.astype(jnp.float32)  9.75 us
    convert_element_type x4, local copies, waits for them, and re-layouts, window_grad(): q_full = q_raw.astype(jnp.float32)  9.66 us
    sub x2, matrix products, window_grad(): attn_probs = jnp.exp(scores - jnp.max(scores, -1, keepdims=True))  8.26 us
    reshape x6, local copies, waits for them, and re-layouts, unwindows(): blocked.reshape(frames // WT, rows // WH, cols // WW, HEADS, WT, WH, WW, HD)  8.2 us
  transfers between devices with their start and end apart: 4, of which 3 were waited for; matrix products, arithmetic and copies ran while one was open for 19% of the time, Pallas kernels for 0%

commit v1 on v0

v1 whole, which is shorter than its diff:
```python
import functools
import math

import jax
import jax.numpy as jnp
from jax import lax
from jax.experimental import pallas as pl
from jax.experimental.pallas import tpu as pltpu
from jax.sharding import PartitionSpec as P

HEADS = 12
HD = 128
WT = 2
WH = 8
WW = 16
HALF_H = WH // 2
TOKENS = WT * WH * WW
HALF_HEADS = HEADS // 2
GAIN_ROWS = 2 * 2 * HEADS

EPSILON = 1e-06
SCALE = HD ** (-0.5)
EXP2_SCALE = SCALE * math.log2(math.e)

MESH = pl.DeviceIdType.MESH
NT = (((1,), (1,)), ((), ()))
NN = (((1,), (0,)), ((), ()))
TN = (((0,), (0,)), ((), ()))


def matmul(a, b, dims):
    return lax.dot_general(a, b, dims, preferred_element_type=jnp.float32)


def head_grad(q_raw, k_raw, values_in, out_grad, gain_q, gain_k):
    q_full = q_raw.astype(jnp.float32)
    k_full = k_raw.astype(jnp.float32)
    inv_q = lax.rsqrt(jnp.mean(q_full * q_full, -1, keepdims=True) + EPSILON)
    inv_k = lax.rsqrt(jnp.mean(k_full * k_full, -1, keepdims=True) + EPSILON)
    unit_q = q_full * inv_q
    unit_k = k_full * inv_k
    q_norm = (unit_q * gain_q).astype(jnp.bfloat16)
    k_norm = (unit_k * gain_k).astype(jnp.bfloat16)
    scores = matmul(k_norm, q_norm, NT)
    prob_grad = matmul(values_in, out_grad, NT)
    top = jnp.max(scores, 0, keepdims=True)
    probs = jnp.exp2((scores - top) * EXP2_SCALE)
    probs = probs * (1.0 / jnp.sum(probs, 0, keepdims=True))
    delta = jnp.sum(probs * prob_grad, 0, keepdims=True)
    score_grad = (probs * (prob_grad - delta)).astype(jnp.bfloat16)
    value_grad = matmul(probs.astype(jnp.bfloat16), out_grad, NN).astype(jnp.bfloat16)
    kn_grad = matmul(score_grad, q_norm, NN)
    qn_grad = matmul(score_grad, k_norm, TN)

    def raw_grad(norm_grad, unit, inverse, gain):
        along = norm_grad * unit
        gain_grad = jnp.sum(along, 0, keepdims=True) * SCALE
        scaled_gain = gain * SCALE
        mean = jnp.mean(along * scaled_gain, -1, keepdims=True)
        raw = inverse * (norm_grad * scaled_gain - unit * mean)
        return raw.astype(jnp.bfloat16), gain_grad

    q_grad, gain_q_grad = raw_grad(qn_grad, unit_q, inv_q, gain_q)
    k_grad, gain_k_grad = raw_grad(kn_grad, unit_k, inv_k, gain_k)
    return (q_grad, k_grad, value_grad), gain_q_grad, gain_k_grad


def kernel(
    n_t, n_h,
    saved, gains, out, gain_out,
    x0, x1, y0, y1, part, piece_in, piece_mid, total,
    load0, load1, store0, store1,
    in_send, in_recv, out_send, out_recv, gain_send, gain_recv,
):
    t = lax.axis_index("tm")
    h = lax.axis_index("height")
    rows = GAIN_ROWS // n_h

    def t_at(shift):
        return lax.rem(t + shift + n_t, n_t)

    def h_at(shift):
        return lax.rem(h + shift + n_h, n_h)

    def features(head):
        return pl.ds(pl.multiple_of(head * HD, HD), HD)

    def unit(u):
        role = lax.rem(u, 2)
        return role, role * HALF_HEADS + u // 2

    def quadrant(u, slot):
        role, head = unit(u)
        frame = 1 - role if slot < 2 else role
        first = HALF_H if slot % 2 == 0 else 0
        return frame, pl.ds(first, HALF_H), head

    def owner(u, slot):
        role, _ = unit(u)
        shift = 0 if slot < 2 else 1 - 2 * role
        return (t_at(shift), h_at(slot % 2))

    def worker(u, slot):
        role, _ = unit(u)
        shift = 0 if slot < 2 else 2 * role - 1
        return (t_at(shift), h_at(-(slot % 2)))

    def in_copy(u, slot):
        frame, band, head = quadrant(u, slot)
        return pltpu.make_async_remote_copy(
            src_ref=saved.at[1, :, frame, band, :, features(head)],
            dst_ref=x1.at[u, :, slot],
            send_sem=in_send.at[u, slot - 1],
            recv_sem=in_recv.at[u, slot - 1],
            device_id=worker(u, slot),
            device_id_type=MESH,
        )

    def in_local(u):
        frame, band, head = quadrant(u, 0)
        return pltpu.make_async_copy(
            saved.at[1, :, frame, band, :, features(head)], x1.at[u, :, 0], load1.at[u]
        )

    def out_copy(u, slot):
        frame, band, head = quadrant(u, slot)
        return pltpu.make_async_remote_copy(
            src_ref=y1.at[u, :, slot],
            dst_ref=out.at[1, :, frame, band, :, features(head)],
            send_sem=out_send.at[u, slot - 1],
            recv_sem=out_recv.at[u, slot - 1],
            device_id=owner(u, slot),
            device_id_type=MESH,
        )

    def out_local(u):
        frame, band, head = quadrant(u, 0)
        return pltpu.make_async_copy(
            y1.at[u, :, 0], out.at[1, :, frame, band, :, features(head)], store1.at[u]
        )

    def load(head):
        return pltpu.make_async_copy(
            saved.at[0, :, :, :, :, features(head)], x0.at[head], load0.at[head]
        )

    def store(head):
        return pltpu.make_async_copy(
            y0.at[head], out.at[0, :, :, :, :, features(head)], store0.at[head]
        )

    def each(count, body):
        lax.fori_loop(0, count, lambda i, carry: (body(i), carry)[1], 0)

    def start_local(u):
        load(u).start()
        in_local(u).start()

    each(HEADS, start_local)
    barrier = pltpu.get_barrier_semaphore()

    def greet(t_to, h_to):
        pl.semaphore_signal(barrier, inc=1, device_id=(t_to, h_to), device_id_type=MESH)

    for dt in (-1, 1):
        for dh in (-1, 1):
            greet(t_at(dt), h_at(dh))
    each(n_h - 1, lambda i: greet(t, h_at(i + 1)))
    each(n_t - 1, lambda i: greet(t_at(i + 1), h))
    pl.semaphore_wait(barrier, 4 + (n_h - 1) + (n_t - 1))

    def start_inputs(u):
        for slot in (2, 3, 1):
            in_copy(u, slot).start()

    each(HEADS, start_inputs)

    def compute(source, target, index, block, head):
        operands = [source[index, a].reshape(TOKENS, HD) for a in range(4)]
        gain_q = gains[block, head, 0:1, :]
        gain_k = gains[block, head, 1:2, :]
        grads, gain_q_grad, gain_k_grad = head_grad(*operands, gain_q, gain_k)
        for a in range(3):
            target[index, a] = grads[a].reshape(target.shape[2:])
        row = 2 * (block * HEADS + head)
        part[row] = gain_q_grad
        part[row + 1] = gain_k_grad

    def step(u):
        load(u).wait()
        compute(x0, y0, u, 0, u)
        store(u).start()
        in_local(u).wait()
        for slot in (1, 2, 3):
            in_copy(u, slot).wait_recv()
        compute(x1, y1, u, 1, unit(u)[1])
        for slot in (2, 3, 1):
            out_copy(u, slot).start()
        out_local(u).start()

    each(HEADS, step)

    def piece(index):
        return pl.ds(index * rows, rows)

    def scatter(k):
        return pltpu.make_async_remote_copy(
            src_ref=part.at[piece(h_at(k))],
            dst_ref=piece_in.at[h],
            send_sem=gain_send.at[0, k],
            recv_sem=gain_recv.at[0, k],
            device_id=(t, h_at(k)),
            device_id_type=MESH,
        )

    def exchange(k):
        return pltpu.make_async_remote_copy(
            src_ref=piece_mid.at[t],
            dst_ref=piece_mid.at[t],
            send_sem=gain_send.at[1, k],
            recv_sem=gain_recv.at[1, k],
            device_id=(t_at(k), h),
            device_id_type=MESH,
        )

    def gather(k):
        return pltpu.make_async_remote_copy(
            src_ref=total.at[piece(h)],
            dst_ref=total.at[piece(h)],
            send_sem=gain_send.at[2, k],
            recv_sem=gain_recv.at[2, k],
            device_id=(t, h_at(k)),
            device_id_type=MESH,
        )

    each(n_h - 1, lambda i: scatter(i + 1).start())
    piece_in[h] = part[piece(h)]
    each(n_h - 1, lambda i: scatter(i + 1).wait_recv())
    piece_mid[t] = jnp.sum(piece_in[...], 0)
    each(n_t - 1, lambda i: exchange(i + 1).start())
    each(n_t - 1, lambda i: exchange(i + 1).wait_recv())
    total[piece(h)] = jnp.sum(piece_mid[...], 0)
    each(n_h - 1, lambda i: gather(i + 1).start())
    each(n_h - 1, lambda i: gather(i + 1).wait_recv())
    for row in range(GAIN_ROWS):
        block, rest = divmod(row, 2 * HEADS)
        head, side = divmod(rest, 2)
        gain_out[block, head, side : side + 1, :] = total[row]
    each(n_h - 1, lambda i: scatter(i + 1).wait_send())
    each(n_t - 1, lambda i: exchange(i + 1).wait_send())
    each(n_h - 1, lambda i: gather(i + 1).wait_send())

    def finish(u):
        store(u).wait()
        out_local(u).wait()
        for slot in (1, 2, 3):
            in_copy(u, slot).wait_send()
            out_copy(u, slot).wait()

    each(HEADS, finish)


def solution(mesh):
    n_t, n_h = mesh.shape["tm"], mesh.shape["height"]
    rows = GAIN_ROWS // n_h
    dma = pltpu.SemaphoreType.DMA

    def shards(saved, gains):
        grads_shape = (2, 3) + saved.shape[2:]
        half_window = (HALF_H, WW, HD)
        grads, gain_grads = pl.pallas_call(
            functools.partial(kernel, n_t, n_h),
            out_shape=(
                jax.ShapeDtypeStruct(grads_shape, jnp.bfloat16),
                jax.ShapeDtypeStruct((2, HEADS, 2, HD), jnp.float32),
            ),
            in_specs=[
                pl.BlockSpec(memory_space=pl.ANY),
                pl.BlockSpec(memory_space=pltpu.VMEM),
            ],
            out_specs=(
                pl.BlockSpec(memory_space=pl.ANY),
                pl.BlockSpec(memory_space=pltpu.VMEM),
            ),
            scratch_shapes=[
                pltpu.VMEM((HEADS, 4, WT, WH, WW, HD), jnp.bfloat16),
                pltpu.VMEM((HEADS, 4, 4) + half_window, jnp.bfloat16),
                pltpu.VMEM((HEADS, 3, WT, WH, WW, HD), jnp.bfloat16),
                pltpu.VMEM((HEADS, 3, 4) + half_window, jnp.bfloat16),
                pltpu.VMEM((GAIN_ROWS, 1, HD), jnp.float32),
                pltpu.VMEM((n_h, rows, 1, HD), jnp.float32),
                pltpu.VMEM((n_t, rows, 1, HD), jnp.float32),
                pltpu.VMEM((GAIN_ROWS, 1, HD), jnp.float32),
                dma((HEADS,)),
                dma((HEADS,)),
                dma((HEADS,)),
                dma((HEADS,)),
                dma((HEADS, 3)),
                dma((HEADS, 3)),
                dma((HEADS, 3)),
                dma((HEADS, 3)),
                dma((3, max(n_t, n_h))),
                dma((3, max(n_t, n_h))),
            ],
            compiler_params=pltpu.CompilerParams(
                collective_id=0, has_side_effects=True, vmem_limit_bytes=56 * 2**20
            ),
            cost_estimate=pl.CostEstimate(
                flops=2 * HEADS * 5 * 2 * TOKENS * TOKENS * HD,
                bytes_accessed=14 * HEADS * TOKENS * HD * 2,
                transcendentals=2 * HEADS * TOKENS * TOKENS,
            ),
        )(saved, gains.transpose(0, 2, 1, 3))
        return grads, gain_grads.transpose(0, 2, 1, 3)

    return jax.shard_map(
        shards,
        mesh=mesh,
        in_specs=(P(None, None, "tm", "height", None, None), P()),
        out_specs=(P(None, None, "tm", "height", None, None), P()),
        check_vma=False,
    )
```

time: 269 us -> 68.1 us (0.25)
  blocking collectives: 76.8 us -> 0 us
  local copies, waits for them, and re-layouts: 75 us -> 5.46 us
  Pallas kernels: 0 us -> 61.8 us
  waiting for transfers between devices: 38.1 us -> 0 us
  other arithmetic: 36.1 us -> 0 us
  matrix products: 30.1 us -> 0 us
  starting transfers between devices: 10.9 us -> 0 us
    psum x1 -> x0, blocking collectives: 76.8 us -> none  [shards(): gains_one, gains_zero = lax.psum((gains_one, gains_zero), ('tm', 'height'))]
    pallas_call x0 -> x1, Pallas kernels: none -> 61.8 us  [shards(): pl.pallas_call(functools.partial(kernel, n_t, n_h), out_shape=(jax.ShapeD...]
    ppermute x4 -> x0, waiting for transfers between devices: 38.1 us -> none  [from_behind(): return lax.ppermute(block, axis, route)]
    dot_general x8 -> x0, matrix products: 21.8 us -> none  [the longest x2 6.99 us: window_grad(): jnp.einsum('nhqk,nhkd->nhqd', score_grad, k_norm, preferred_element_type=...]
    another operation x15 -> x0, local copies, waits for them, and re-layouts: 21.5 us -> none  [the longest x7 13.4 us: block_grad(): jnp.stack([unwindows(results[index], layout) for index in range(3)])]
    convert_element_type x8 -> x0, local copies, waits for them, and re-layouts: 19.4 us -> none  [the longest x4 9.75 us: window_grad(): k_full = k_raw.astype(jnp.float32)]
    ppermute x4 -> x0, starting transfers between devices: 10.9 us -> none  [from_behind(): return lax.ppermute(block, axis, route)]
    convert_element_type x7 -> x0, other arithmetic: 10.3 us -> none  [the longest x4 5.61 us: raw_grad(): (inverse * (scaled - unit * jnp.mean(scaled * unit, -1, keepdims=True)))....]
  transfers between devices with their start and end apart: 4 -> 0, of which waited for: 3 -> 0; matrix products, arithmetic and copies ran while one was open for 19% -> 0% of each run, Pallas kernels for 0% -> 0%
where the time goes in v1:
time: 68.1 us; the launch traced here: 67.9 us
  Pallas kernels  61.8 us (91%)
  local copies, waits for them, and re-layouts  5.46 us (8%)
    pallas_call x1, Pallas kernels, shards(): pl.pallas_call(functools.partial(kernel, n_t, n_h), out_shape=(jax.ShapeD...  61.8 us
    unnamed x4, local copies, waits for them, and re-layouts  5.46 us

profile of v1, /device:TPU:1, one launch (start us, length us, event | category | flops | bytes accessed | tf_op | source)
XLA Modules:
  0.0 67.9 jit_solution(4959121503999460636)
XLA Ops:
  0.6 61.8 %shard_map.41 = (bf16[2,3,2,8,16,1536]{5,4,3,2,1,0:T(8,128)(2,1)}, f32[2,12,2,128]{3,2,1,0:T(2,128)}) custom-call(bf16[2,4,2,8,16,1536]{5,4,3,2,1,0:T(8,128)(2,1)} %saved.1, f32[2,12,2,128]{3,2,1,0:T(2,128)} %bitcast.3), custom_call_target="tpu_custom_call" | custom-call | flops 2013265920 | bytes 11010048 | tf_op jit(solution)/shard_map/pallas_call | solution.py:271
  62.4 0.0 copy-start
  62.5 4.8 %copy.6 = bf16[2,3,2,8,16,1536]{5,4,3,2,1,0:T(8,128)(2,1)} copy(bf16[2,3,2,8,16,1536]{5,4,3,2,1,0:T(8,128)(2,1)} %get-tuple-element.8) | data formatting | bytes 9437184
  67.3 0.0 copy-done
  67.3 0.6 copy.7
Async XLA Ops:
  62.4 4.9 %copy-start = (f32[2,12,2,128]{3,2,1,0:T(2,128)S(1)}, f32[2,12,2,128]{3,2,1,0:T(2,128)}, u32[]{:S(2)}) copy-start(f32[2,12,2,128]{3,2,1,0:T(2,128)} %get-tuple-element.5) | copy-start | bytes 73732

commit v2 on v1

v2 whole, which is shorter than its diff:
```python
import functools
import math

import jax
import jax.numpy as jnp
from jax import lax
from jax.experimental import pallas as pl
from jax.experimental.pallas import tpu as pltpu
from jax.sharding import PartitionSpec as P

HEADS = 12
HD = 128
WT = 2
WH = 8
WW = 16
HALF_H = WH // 2
TOKENS = WT * WH * WW
ROLES = 4

EPSILON = 1e-06
SCALE = HD ** (-0.5)
EXP2_SCALE = SCALE * math.log2(math.e)

MESH = pl.DeviceIdType.MESH
NT = (((1,), (1,)), ((), ()))
NN = (((1,), (0,)), ((), ()))
TN = (((0,), (0,)), ((), ()))


def matmul(a, b, dims):
    return lax.dot_general(a, b, dims, preferred_element_type=jnp.float32)


def head_grad(q_raw, k_raw, values_in, out_grad, gain_q, gain_k):
    q_full = q_raw.astype(jnp.float32)
    k_full = k_raw.astype(jnp.float32)
    inv_q = lax.rsqrt(jnp.mean(q_full * q_full, -1, keepdims=True) + EPSILON)
    inv_k = lax.rsqrt(jnp.mean(k_full * k_full, -1, keepdims=True) + EPSILON)
    unit_q = q_full * inv_q
    unit_k = k_full * inv_k
    q_norm = (unit_q * gain_q).astype(jnp.bfloat16)
    k_norm = (unit_k * gain_k).astype(jnp.bfloat16)
    scores = matmul(k_norm, q_norm, NT)
    prob_grad = matmul(values_in, out_grad, NT)
    top = jnp.max(scores, 0, keepdims=True)
    probs = jnp.exp2((scores - top) * EXP2_SCALE)
    probs = probs * (1.0 / jnp.sum(probs, 0, keepdims=True))
    delta = jnp.sum(probs * prob_grad, 0, keepdims=True)
    score_grad = (probs * (prob_grad - delta)).astype(jnp.bfloat16)
    value_grad = matmul(probs.astype(jnp.bfloat16), out_grad, NN).astype(jnp.bfloat16)
    kn_grad = matmul(score_grad, q_norm, NN)
    qn_grad = matmul(score_grad, k_norm, TN)

    def raw_grad(norm_grad, unit, inverse, gain):
        along = norm_grad * unit
        gain_grad = jnp.sum(along, 0, keepdims=True) * SCALE
        scaled_gain = gain * SCALE
        mean = jnp.mean(along * scaled_gain, -1, keepdims=True)
        raw = inverse * (norm_grad * scaled_gain - unit * mean)
        return raw.astype(jnp.bfloat16), gain_grad

    q_grad, gain_q_grad = raw_grad(qn_grad, unit_q, inv_q, gain_q)
    k_grad, gain_k_grad = raw_grad(kn_grad, unit_k, inv_k, gain_k)
    return (q_grad, k_grad, value_grad), gain_q_grad, gain_k_grad


def each(count, body):
    lax.fori_loop(0, count, lambda i, carry: (body(i), carry)[1], 0)


def groups(size):
    low = min(size, 4)
    return (1, low), (low, size // low)


def grad_kernel(
    n_t, n_h,
    saved, gains_far, grads, gain_grads,
    x0, x1, w1, gains, sums, stages, totals,
    load_gains, load0, load1, in_send, in_recv, out_send, out_recv, sum_send, sum_recv,
):
    t = lax.axis_index("tm")
    h = lax.axis_index("height")

    def at(dt, dh):
        return (lax.rem(t + dt + n_t, n_t), lax.rem(h + dh + n_h, n_h))

    def features(head):
        return pl.ds(pl.multiple_of(head * HD, HD), HD)

    def unit(u):
        role = lax.rem(u, ROLES)
        return lax.rem(role, 2), role // 2, role * (HEADS // ROLES) + u // ROLES

    def holder(u, slot):
        rt, rh, _ = unit(u)
        return (rt if slot < 2 else 1 - rt), (rh if slot % 2 == 0 else 1 - rh)

    def quadrant(u, slot):
        a, b = holder(u, slot)
        return 1 - a, pl.ds((1 - b) * HALF_H, HALF_H), slice(None), features(unit(u)[2])

    def owner(u, slot):
        (rt, rh, _), (a, b) = unit(u), holder(u, slot)
        return at(a - rt, b - rh)

    def worker(u, slot):
        (rt, rh, _), (a, b) = unit(u), holder(u, slot)
        return at(rt - a, rh - b)

    def in_copy(u, slot):
        return pltpu.make_async_remote_copy(
            src_ref=saved.at[(1, slice(None)) + quadrant(u, slot)],
            dst_ref=x1.at[u, :, slot],
            send_sem=in_send.at[u, slot - 1],
            recv_sem=in_recv.at[u, slot - 1],
            device_id=worker(u, slot),
            device_id_type=MESH,
        )

    def in_local(u):
        return pltpu.make_async_copy(
            saved.at[(1, slice(None)) + quadrant(u, 0)], x1.at[u, :, 0], load1.at[u]
        )

    def out_copy(u, slot):
        return pltpu.make_async_remote_copy(
            src_ref=w1.at[u, :, slot - 1],
            dst_ref=grads.at[(1, slice(None)) + quadrant(u, slot)],
            send_sem=out_send.at[u, slot - 1],
            recv_sem=out_recv.at[u, slot - 1],
            device_id=owner(u, slot),
            device_id_type=MESH,
        )

    def load(a):
        return pltpu.make_async_copy(saved.at[0, a], x0.at[a], load0.at[a])

    (h_low, h_high), (t_low, t_high) = groups(n_h), groups(n_t)
    plan = [("height",) + h_low, ("height",) + h_high, ("tm",) + t_low, ("tm",) + t_high]

    def place(axis, stride, count):
        return lax.rem((h if axis == "height" else t) // stride, count)

    def peer(axis, stride, count, k):
        mine = place(axis, stride, count)
        other = lax.rem(mine + k, count)
        shift = (other - mine) * stride
        return other, (at(0, shift) if axis == "height" else at(shift, 0))

    gains_copy = pltpu.make_async_copy(gains_far, gains, load_gains)
    gains_copy.start()
    each(4, lambda a: load(a).start())
    each(HEADS, lambda u: in_local(u).start())

    barrier = pltpu.get_barrier_semaphore()

    def greet(device):
        pl.semaphore_signal(barrier, inc=1, device_id=device, device_id_type=MESH)

    greeted = 0
    for dt in (-1, 0, 1):
        for dh in (-1, 0, 1):
            if dt or dh:
                greet(at(dt, dh))
                greeted += 1
    for group in plan:
        for k in range(1, group[2]):
            greet(peer(*group, k)[1])
            greeted += 1
    pl.semaphore_wait(barrier, greeted)

    def start_inputs(u):
        for slot in (2, 3, 1):
            in_copy(u, slot).start()

    each(HEADS, start_inputs)
    gains_copy.wait()
    each(4, lambda a: load(a).wait())

    def compute(operands, block, head):
        results, gain_q_grad, gain_k_grad = head_grad(
            *(x.reshape(TOKENS, HD) for x in operands),
            gains[block, head, 0:1, :],
            gains[block, head, 1:2, :],
        )
        sums[block * HEADS + head, 0:1, :] = gain_q_grad
        sums[block * HEADS + head, 1:2, :] = gain_k_grad
        return results

    def step(u):
        results = compute([x0[a, :, :, :, features(u)] for a in range(4)], 0, u)
        for a in range(3):
            grads[0, a, :, :, :, features(u)] = results[a].reshape(WT, WH, WW, HD)
        in_local(u).wait()
        for slot in (1, 2, 3):
            in_copy(u, slot).wait_recv()
        results = compute([x1[u, a] for a in range(4)], 1, unit(u)[2])
        for a in range(3):
            quads = results[a].reshape(4, HALF_H, WW, HD)
            w1[u, a] = quads[1:]
            grads[(1, a) + quadrant(u, 0)] = quads[0]
        for slot in (2, 3, 1):
            out_copy(u, slot).start()

    each(HEADS, step)

    size = 2 * HEADS // h_low[1]

    def sum_copy(index, k):
        other, device = peer(*plan[index % 4], k)
        mine = place(*plan[index % 4])
        if index == 0:
            source, target = sums.at[pl.ds(other * size, size)], stages.at[0, mine]
        elif index < 4:
            source = target = stages.at[index, mine]
        else:
            source = target = totals.at[pl.ds(mine * size, size)]
        return pltpu.make_async_remote_copy(
            src_ref=source,
            dst_ref=target,
            send_sem=sum_send.at[index, k],
            recv_sem=sum_recv.at[index, k],
            device_id=device,
            device_id_type=MESH,
        )

    here = pl.ds(place(*plan[0]) * size, size)
    for index in range(5):
        count = plan[index % 4][2]
        if index == 0:
            value = sums[here]
        if index < 4:
            stages[index, place(*plan[index])] = value
        else:
            totals[here] = value
        for k in range(1, count):
            sum_copy(index, k).start()
        for k in range(1, count):
            sum_copy(index, k).wait_recv()
        if index < 4:
            value = functools.reduce(jnp.add, [stages[index, i] for i in range(count)])
    gain_grads[...] = totals[...].reshape(2, HEADS, 2, HD)
    for index in range(5):
        for k in range(1, plan[index % 4][2]):
            sum_copy(index, k).wait_send()

    def finish(u):
        for slot in (1, 2, 3):
            in_copy(u, slot).wait_send()
            out_copy(u, slot).wait()

    each(HEADS, finish)


def write_kernel(grads_in, sums_in, grads, sums, sem):
    def write(index):
        block, a = index // 3, lax.rem(index, 3)
        return pltpu.make_async_copy(grads_in.at[block, a], grads.at[block, a], sem.at[index])

    each(6, lambda index: write(index).start())
    sums[...] = sums_in[...]
    each(6, lambda index: write(index).wait())


def solution(mesh):
    n_t, n_h = mesh.shape["tm"], mesh.shape["height"]
    dma = pltpu.SemaphoreType.DMA
    far = pl.BlockSpec(memory_space=pl.ANY)
    near = pl.BlockSpec(memory_space=pltpu.VMEM)
    quads = (4, HALF_H, WW, HD)
    gain_shape = jax.ShapeDtypeStruct((2, HEADS, 2, HD), jnp.float32)

    def shards(saved, gains):
        saved = pltpu.with_memory_space_constraint(saved, pltpu.HBM)
        gains = pltpu.with_memory_space_constraint(gains.transpose(0, 2, 1, 3), pltpu.HBM)
        grads_shape = (2, 3) + saved.shape[2:]
        grads, gain_grads = pl.pallas_call(
            functools.partial(grad_kernel, n_t, n_h),
            out_shape=(pltpu.VMEM(grads_shape, jnp.bfloat16), gain_shape),
            in_specs=[far, far],
            out_specs=(near, near),
            scratch_shapes=[
                pltpu.VMEM(saved.shape[1:], jnp.bfloat16),
                pltpu.VMEM((HEADS, 4) + quads, jnp.bfloat16),
                pltpu.VMEM((HEADS, 3, 3) + quads[1:], jnp.bfloat16),
                pltpu.VMEM((2, HEADS, 2, HD), jnp.float32),
                pltpu.VMEM((2 * HEADS, 2, HD), jnp.float32),
                pltpu.VMEM((4, 4, 2 * HEADS // min(n_h, 4), 2, HD), jnp.float32),
                pltpu.VMEM((2 * HEADS, 2, HD), jnp.float32),
                dma,
                dma((4,)),
                dma((HEADS,)),
                dma((HEADS, 3)),
                dma((HEADS, 3)),
                dma((HEADS, 3)),
                dma((HEADS, 3)),
                dma((5, 4)),
                dma((5, 4)),
            ],
            compiler_params=pltpu.CompilerParams(
                collective_id=0, has_side_effects=True, vmem_limit_bytes=40 * 2**20
            ),
        )(saved, gains)
        grads, gain_grads = pl.pallas_call(
            write_kernel,
            out_shape=(jax.ShapeDtypeStruct(grads_shape, jnp.bfloat16), gain_shape),
            in_specs=[near, near],
            out_specs=(far, near),
            scratch_shapes=[dma((6,))],
        )(grads, gain_grads)
        return grads, gain_grads.transpose(0, 2, 1, 3)

    return jax.shard_map(
        shards,
        mesh=mesh,
        in_specs=(P(None, None, "tm", "height", None, None), P()),
        out_specs=(P(None, None, "tm", "height", None, None), P()),
        check_vma=False,
    )
```

time: 68.1 us -> 71.3 us (1.047)
  Pallas kernels: 61.8 us -> 67.6 us
  local copies, waits for them, and re-layouts: 5.46 us -> 2.71 us
    pallas_call x1 -> x2, Pallas kernels: 61.8 us -> 67.6 us  [the longest x1 62.5 us: shards(): pl.pallas_call(functools.partial(grad_kernel, n_t, n_h), out_shape=(pltpu...]
    unnamed x4, local copies, waits for them, and re-layouts: 5.46 us -> 2.71 us
where the time goes in v2:
time: 71.3 us; the launch traced here: 71 us
  Pallas kernels  67.6 us (95%)
  local copies, waits for them, and re-layouts  2.71 us (4%)
    pallas_call x1, Pallas kernels, shards(): pl.pallas_call(functools.partial(grad_kernel, n_t, n_h), out_shape=(pltpu...  62.5 us
    pallas_call x1, Pallas kernels, shards(): pl.pallas_call(write_kernel, out_shape=(jax.ShapeDtypeStruct(grads_shape,...  5.17 us
    unnamed x4, local copies, waits for them, and re-layouts  2.71 us

profile of v2, /device:TPU:1, one launch (start us, length us, event | category | flops | bytes accessed | tf_op | source)
XLA Modules:
  0.0 71.0 jit_solution(2174591705085415831)
XLA Ops:
  0.6 62.5 %shard_map.41 = (bf16[2,3,2,8,16,1536]{5,4,3,2,1,0:T(8,128)(2,1)S(1)}, f32[2,12,2,128]{3,2,1,0:T(2,128)S(1)}) custom-call(bf16[2,4,2,8,16,1536]{5,4,3,2,1,0:T(8,128)(2,1)} %saved.1, f32[2,12,2,128]{3,2,1,0:T(2,128)} %bitcast.2), custom_call_target="tpu_custom_call" | custom-call | tf_op jit(solution)/shard_map/pallas_call | solution.py:278
  63.1 0.0 copy-start
  63.1 2.1 %copy-done = bf16[2,3,2,8,16,1536]{5,4,3,2,1,0:T(8,128)(2,1)} copy-done((bf16[2,3,2,8,16,1536]{5,4,3,2,1,0:T(8,128)(2,1)}, bf16[2,3,2,8,16,1536]{5,4,3,2,1,0:T(8,128)(2,1)S(1)}, u32[]{:S(2)}) %copy-start) | copy-done | bytes 4718616
  65.2 0.0 copy-start.1
  65.2 0.6 copy-done.1
  65.8 5.2 %shard_map.42 = (bf16[2,3,2,8,16,1536]{5,4,3,2,1,0:T(8,128)(2,1)}, f32[2,12,2,128]{3,2,1,0:T(2,128)}) custom-call(bf16[2,3,2,8,16,1536]{5,4,3,2,1,0:T(8,128)(2,1)} %copy-done, f32[2,12,2,128]{3,2,1,0:T(2,128)} %copy-done.1), custom_call_target="tpu_custom_call" | custom-call | tf_op jit(solution)/shard_map/pallas_call | solution.py:305
Async XLA Ops:
  63.1 2.1 %copy-start = (bf16[2,3,2,8,16,1536]{5,4,3,2,1,0:T(8,128)(2,1)}, bf16[2,3,2,8,16,1536]{5,4,3,2,1,0:T(8,128)(2,1)S(1)}, u32[]{:S(2)}) copy-start(bf16[2,3,2,8,16,1536]{5,4,3,2,1,0:T(8,128)(2,1)S(1)} %get-tuple-element.6.grads_in) | copy-start | bytes 14155780
  65.2 0.6 copy-start.1

commit v3 on v2

--- a/solution.py
+++ b/solution.py
@@ -16,6 +16,7 @@
 HALF_H = WH // 2
 TOKENS = WT * WH * WW
 ROLES = 4
+BATCH = 4
 
 EPSILON = 1e-06
 SCALE = HD ** (-0.5)
@@ -200,8 +201,15 @@
             quads = results[a].reshape(4, HALF_H, WW, HD)
             w1[u, a] = quads[1:]
             grads[(1, a) + quadrant(u, 0)] = quads[0]
-        for slot in (2, 3, 1):
-            out_copy(u, slot).start()
+
+        def start_outputs(v):
+            for slot in (2, 3, 1):
+                out_copy(v, slot).start()
+
+        @pl.when(u >= HEADS - HEADS // BATCH)
+        def _():
+            first = (u - (HEADS - HEADS // BATCH)) * BATCH
+            each(BATCH, lambda i: start_outputs(first + i))
 
     each(HEADS, step)
 
@@ -251,16 +259,6 @@
             out_copy(u, slot).wait()
 
     each(HEADS, finish)
-
-
-def write_kernel(grads_in, sums_in, grads, sums, sem):
-    def write(index):
-        block, a = index // 3, lax.rem(index, 3)
-        return pltpu.make_async_copy(grads_in.at[block, a], grads.at[block, a], sem.at[index])
-
-    each(6, lambda index: write(index).start())
-    sums[...] = sums_in[...]
-    each(6, lambda index: write(index).wait())
 
 
 def solution(mesh):
@@ -302,13 +300,6 @@
                 collective_id=0, has_side_effects=True, vmem_limit_bytes=40 * 2**20
             ),
         )(saved, gains)
-        grads, gain_grads = pl.pallas_call(
-            write_kernel,
-            out_shape=(jax.ShapeDtypeStruct(grads_shape, jnp.bfloat16), gain_shape),
-            in_specs=[near, near],
-            out_specs=(far, near),
-            scratch_shapes=[dma((6,))],
-        )(grads, gain_grads)
         return grads, gain_grads.transpose(0, 2, 1, 3)
 
     return jax.shard_map(

time: 71.3 us -> 69.5 us (0.975)
  Pallas kernels: 67.6 us -> 65.8 us
    pallas_call x1 -> x0, Pallas kernels: 5.17 us -> none  [shards(): pl.pallas_call(write_kernel, out_shape=(jax.ShapeDtypeStruct(grads_shape,...]
    pallas_call x1, Pallas kernels: 62.5 us -> 65.8 us  [shards(): pl.pallas_call(functools.partial(grad_kernel, n_t, n_h), out_shape=(pltpu...]
    unnamed x4 -> x2, local copies, waits for them, and re-layouts: 2.71 us -> 2.8 us
where the time goes in v3:
time: 69.5 us; the launch traced here: 69.2 us
  Pallas kernels  65.8 us (95%)
  local copies, waits for them, and re-layouts  2.8 us (4%)
    pallas_call x1, Pallas kernels, shards(): pl.pallas_call(functools.partial(grad_kernel, n_t, n_h), out_shape=(pltpu...  65.8 us
    unnamed x2, local copies, waits for them, and re-layouts  2.8 us

profile of v3, /device:TPU:1, one launch (start us, length us, event | category | flops | bytes accessed | tf_op | source)
XLA Modules:
  0.0 69.2 jit_solution(13499903055070987223)
XLA Ops:
  0.6 65.8 %shard_map.41 = (bf16[2,3,2,8,16,1536]{5,4,3,2,1,0:T(8,128)(2,1)S(1)}, f32[2,12,2,128]{3,2,1,0:T(2,128)S(1)}) custom-call(bf16[2,4,2,8,16,1536]{5,4,3,2,1,0:T(8,128)(2,1)} %saved.1, f32[2,12,2,128]{3,2,1,0:T(2,128)} %bitcast.3), custom_call_target="tpu_custom_call" | custom-call | tf_op jit(solution)/shard_map/pallas_call | solution.py:276
  66.4 2.2 %copy.6 = bf16[2,3,2,8,16,1536]{5,4,3,2,1,0:T(8,128)(2,1)} copy(bf16[2,3,2,8,16,1536]{5,4,3,2,1,0:T(8,128)(2,1)S(1)} %get-tuple-element.6) | data formatting | bytes 9437184
  68.6 0.6 copy.7

commit v4 on v3

--- a/solution.py
+++ b/solution.py
@@ -16,7 +16,8 @@
 HALF_H = WH // 2
 TOKENS = WT * WH * WW
 ROLES = 4
-BATCH = 4
+HELD = 3
+GROUP = 8
 
 EPSILON = 1e-06
 SCALE = HD ** (-0.5)
@@ -69,11 +70,6 @@
     lax.fori_loop(0, count, lambda i, carry: (body(i), carry)[1], 0)
 
 
-def groups(size):
-    low = min(size, 4)
-    return (1, low), (low, size // low)
-
-
 def grad_kernel(
     n_t, n_h,
     saved, gains_far, grads, gain_grads,
@@ -137,17 +133,26 @@
     def load(a):
         return pltpu.make_async_copy(saved.at[0, a], x0.at[a], load0.at[a])
 
-    (h_low, h_high), (t_low, t_high) = groups(n_h), groups(n_t)
-    plan = [("height",) + h_low, ("height",) + h_high, ("tm",) + t_low, ("tm",) + t_high]
-
-    def place(axis, stride, count):
-        return lax.rem((h if axis == "height" else t) // stride, count)
-
-    def peer(axis, stride, count, k):
-        mine = place(axis, stride, count)
-        other = lax.rem(mine + k, count)
-        shift = (other - mine) * stride
-        return other, (at(0, shift) if axis == "height" else at(shift, 0))
+    near_h, near_t = min(n_h, GROUP), min(n_t, GROUP)
+    far_h, far_t = n_h // near_h, n_t // near_t
+    counts = (near_h, far_h * far_t, near_t, near_h)
+
+    def place(stage):
+        if stage == 1:
+            return t // near_t * far_h + h // near_h
+        return lax.rem(t, near_t) if stage == 2 else lax.rem(h, near_h)
+
+    def peer(stage, k):
+        if stage == 1:
+            other_t = lax.rem(t // near_t + k // far_h, far_t)
+            other_h = lax.rem(h // near_h + lax.rem(k, far_h), far_h)
+            return other_t * far_h + other_h, (
+                other_t * near_t + lax.rem(t, near_t),
+                other_h * near_h + lax.rem(h, near_h),
+            )
+        other = lax.rem(place(stage) + k, counts[stage])
+        shift = other - place(stage)
+        return other, ((t + shift, h) if stage == 2 else (t, h + shift))
 
     gains_copy = pltpu.make_async_copy(gains_far, gains, load_gains)
     gains_copy.start()
@@ -165,9 +170,9 @@
             if dt or dh:
                 greet(at(dt, dh))
                 greeted += 1
-    for group in plan:
-        for k in range(1, group[2]):
-            greet(peer(*group, k)[1])
+    for stage in range(3):
+        for k in range(1, counts[stage]):
+            greet(peer(stage, k)[1])
             greeted += 1
     pl.semaphore_wait(barrier, greeted)
 
@@ -188,6 +193,10 @@
         sums[block * HEADS + head, 0:1, :] = gain_q_grad
         sums[block * HEADS + head, 1:2, :] = gain_k_grad
         return results
+
+    def start_outputs(u):
+        for slot in (2, 3, 1):
+            out_copy(u, slot).start()
 
     def step(u):
         results = compute([x0[a, :, :, :, features(u)] for a in range(4)], 0, u)
@@ -202,56 +211,56 @@
             w1[u, a] = quads[1:]
             grads[(1, a) + quadrant(u, 0)] = quads[0]
 
-        def start_outputs(v):
-            for slot in (2, 3, 1):
-                out_copy(v, slot).start()
-
-        @pl.when(u >= HEADS - HEADS // BATCH)
+        @pl.when(u >= HEADS - HELD)
         def _():
-            first = (u - (HEADS - HEADS // BATCH)) * BATCH
-            each(BATCH, lambda i: start_outputs(first + i))
+            start_outputs(2 * (u - HEADS + HELD))
+            start_outputs(2 * (u - HEADS + HELD) + 1)
 
     each(HEADS, step)
 
-    size = 2 * HEADS // h_low[1]
-
-    def sum_copy(index, k):
-        other, device = peer(*plan[index % 4], k)
-        mine = place(*plan[index % 4])
-        if index == 0:
+    size = 2 * HEADS // near_h
+
+    def sum_copy(stage, k):
+        other, device = peer(stage, k)
+        mine = place(stage)
+        if stage == 0:
             source, target = sums.at[pl.ds(other * size, size)], stages.at[0, mine]
-        elif index < 4:
-            source = target = stages.at[index, mine]
+        elif stage < 3:
+            source = target = stages.at[stage, mine]
         else:
             source = target = totals.at[pl.ds(mine * size, size)]
         return pltpu.make_async_remote_copy(
             src_ref=source,
             dst_ref=target,
-            send_sem=sum_send.at[index, k],
-            recv_sem=sum_recv.at[index, k],
+            send_sem=sum_send.at[stage, k],
+            recv_sem=sum_recv.at[stage, k],
             device_id=device,
             device_id_type=MESH,
         )
 
-    here = pl.ds(place(*plan[0]) * size, size)
-    for index in range(5):
-        count = plan[index % 4][2]
-        if index == 0:
-            value = sums[here]
-        if index < 4:
-            stages[index, place(*plan[index])] = value
+    here = pl.ds(place(0) * size, size)
+    value = sums[here]
+    sent = 2 * HELD
+    for stage in range(4):
+        count = counts[stage]
+        if stage < 3:
+            stages[stage, place(stage)] = value
         else:
             totals[here] = value
         for k in range(1, count):
-            sum_copy(index, k).start()
+            sum_copy(stage, k).start()
+        batch = -(-(HEADS - sent) // (4 - stage))
+        for u in range(sent, sent + batch):
+            start_outputs(u)
+        sent += batch
         for k in range(1, count):
-            sum_copy(index, k).wait_recv()
-        if index < 4:
-            value = functools.reduce(jnp.add, [stages[index, i] for i in range(count)])
+            sum_copy(stage, k).wait_recv()
+        if stage < 3:
+            value = functools.reduce(jnp.add, [stages[stage, i] for i in range(count)])
     gain_grads[...] = totals[...].reshape(2, HEADS, 2, HD)
-    for index in range(5):
-        for k in range(1, plan[index % 4][2]):
-            sum_copy(index, k).wait_send()
+    for stage in range(4):
+        for k in range(1, counts[stage]):
+            sum_copy(stage, k).wait_send()
 
     def finish(u):
         for slot in (1, 2, 3):
@@ -284,7 +293,7 @@
                 pltpu.VMEM((HEADS, 3, 3) + quads[1:], jnp.bfloat16),
                 pltpu.VMEM((2, HEADS, 2, HD), jnp.float32),
                 pltpu.VMEM((2 * HEADS, 2, HD), jnp.float32),
-                pltpu.VMEM((4, 4, 2 * HEADS // min(n_h, 4), 2, HD), jnp.float32),
+                pltpu.VMEM((3, GROUP, 2 * HEADS // min(n_h, GROUP), 2, HD), jnp.float32),
                 pltpu.VMEM((2 * HEADS, 2, HD), jnp.float32),
                 dma,
                 dma((4,)),
@@ -293,8 +302,8 @@
                 dma((HEADS, 3)),
                 dma((HEADS, 3)),
                 dma((HEADS, 3)),
-                dma((5, 4)),
-                dma((5, 4)),
+                dma((4, GROUP)),
+                dma((4, GROUP)),
             ],
             compiler_params=pltpu.CompilerParams(
                 collective_id=0, has_side_effects=True, vmem_limit_bytes=40 * 2**20

time: 69.5 us -> 64.7 us (0.931)
  Pallas kernels: 65.8 us -> 60.5 us
    pallas_call x1, Pallas kernels: 65.8 us -> 60.5 us  [shards(): pl.pallas_call(functools.partial(grad_kernel, n_t, n_h), out_shape=(pltpu...]
where the time goes in v4:
time: 64.7 us; the launch traced here: 63.9 us
  Pallas kernels  60.5 us (94%)
  local copies, waits for them, and re-layouts  2.8 us (4%)
    pallas_call x1, Pallas kernels, shards(): pl.pallas_call(functools.partial(grad_kernel, n_t, n_h), out_shape=(pltpu...  60.5 us
    unnamed x2, local copies, waits for them, and re-layouts  2.8 us

profile of v4, /device:TPU:1, one launch (start us, length us, event | category | flops | bytes accessed | tf_op | source)
XLA Modules:
  0.0 63.9 jit_solution(10961771034208519526)
XLA Ops:
  0.6 60.5 %shard_map.41 = (bf16[2,3,2,8,16,1536]{5,4,3,2,1,0:T(8,128)(2,1)S(1)}, f32[2,12,2,128]{3,2,1,0:T(2,128)S(1)}) custom-call(bf16[2,4,2,8,16,1536]{5,4,3,2,1,0:T(8,128)(2,1)} %saved.1, f32[2,12,2,128]{3,2,1,0:T(2,128)} %bitcast.3), custom_call_target="tpu_custom_call" | custom-call | tf_op jit(solution)/shard_map/pallas_call | solution.py:285
  61.1 2.2 %copy.6 = bf16[2,3,2,8,16,1536]{5,4,3,2,1,0:T(8,128)(2,1)} copy(bf16[2,3,2,8,16,1536]{5,4,3,2,1,0:T(8,128)(2,1)S(1)} %get-tuple-element.6) | data formatting | bytes 9437184
  63.3 0.6 copy.7

commit v5 on v4

--- a/solution.py
+++ b/solution.py
@@ -16,7 +16,6 @@
 HALF_H = WH // 2
 TOKENS = WT * WH * WW
 ROLES = 4
-HELD = 3
 GROUP = 8
 
 EPSILON = 1e-06
@@ -198,6 +197,13 @@
         for slot in (2, 3, 1):
             out_copy(u, slot).start()
 
+    def wait_outputs(u):
+        for slot in (2, 3, 1):
+            out_copy(u, slot).wait_send()
+
+    edge = lax.rem(t, min(n_t, GROUP))
+    held = jnp.logical_or(edge == 0, edge == min(n_t, GROUP) - 1)
+
     def step(u):
         results = compute([x0[a, :, :, :, features(u)] for a in range(4)], 0, u)
         for a in range(3):
@@ -211,10 +217,9 @@
             w1[u, a] = quads[1:]
             grads[(1, a) + quadrant(u, 0)] = quads[0]
 
-        @pl.when(u >= HEADS - HELD)
+        @pl.when(jnp.logical_not(held))
         def _():
-            start_outputs(2 * (u - HEADS + HELD))
-            start_outputs(2 * (u - HEADS + HELD) + 1)
+            start_outputs(u)
 
     each(HEADS, step)
 
@@ -240,7 +245,7 @@
 
     here = pl.ds(place(0) * size, size)
     value = sums[here]
-    sent = 2 * HELD
+    batch = HEADS // 4
     for stage in range(4):
         count = counts[stage]
         if stage < 3:
@@ -249,10 +254,19 @@
             totals[here] = value
         for k in range(1, count):
             sum_copy(stage, k).start()
-        batch = -(-(HEADS - sent) // (4 - stage))
-        for u in range(sent, sent + batch):
-            start_outputs(u)
-        sent += batch
+
+        @pl.when(held)
+        def _():
+            def send(i):
+                u = stage * batch + i
+                start_outputs(u)
+
+                @pl.when(u > 0)
+                def _():
+                    wait_outputs(u - 1)
+
+            each(batch, send)
+
         for k in range(1, count):
             sum_copy(stage, k).wait_recv()
         if stage < 3:
@@ -265,7 +279,11 @@
     def finish(u):
         for slot in (1, 2, 3):
             in_copy(u, slot).wait_send()
-            out_copy(u, slot).wait()
+            out_copy(u, slot).wait_recv()
+
+        @pl.when(jnp.logical_or(jnp.logical_not(held), u == HEADS - 1))
+        def _():
+            wait_outputs(u)
 
     each(HEADS, finish)
 

time: 64.7 us -> 67.2 us (1.039)
  Pallas kernels: 60.5 us -> 63.5 us
    pallas_call x1, Pallas kernels: 60.5 us -> 63.5 us  [shards(): pl.pallas_call(functools.partial(grad_kernel, n_t, n_h), out_shape=(pltpu...]
where the time goes in v5:
time: 67.2 us; the launch traced here: 66.9 us
  Pallas kernels  63.5 us (94%)
  local copies, waits for them, and re-layouts  2.8 us (4%)
    pallas_call x1, Pallas kernels, shards(): pl.pallas_call(functools.partial(grad_kernel, n_t, n_h), out_shape=(pltpu...  63.5 us
    unnamed x2, local copies, waits for them, and re-layouts  2.8 us

profile of v5, /device:TPU:1, one launch (start us, length us, event | category | flops | bytes accessed | tf_op | source)
XLA Modules:
  0.0 66.9 jit_solution(18012189377496832618)
XLA Ops:
  0.6 63.5 %shard_map.41 = (bf16[2,3,2,8,16,1536]{5,4,3,2,1,0:T(8,128)(2,1)S(1)}, f32[2,12,2,128]{3,2,1,0:T(2,128)S(1)}) custom-call(bf16[2,4,2,8,16,1536]{5,4,3,2,1,0:T(8,128)(2,1)} %saved.1, f32[2,12,2,128]{3,2,1,0:T(2,128)} %bitcast.3), custom_call_target="tpu_custom_call" | custom-call | tf_op jit(solution)/shard_map/pallas_call | solution.py:303
  64.1 2.2 %copy.6 = bf16[2,3,2,8,16,1536]{5,4,3,2,1,0:T(8,128)(2,1)} copy(bf16[2,3,2,8,16,1536]{5,4,3,2,1,0:T(8,128)(2,1)S(1)} %get-tuple-element.6) | data formatting | bytes 9437184
  66.3 0.6 copy.7

commit v6 on v5

--- a/solution.py
+++ b/solution.py
@@ -15,6 +15,7 @@
 WW = 16
 HALF_H = WH // 2
 TOKENS = WT * WH * WW
+PART = 128
 ROLES = 4
 GROUP = 8
 
@@ -33,24 +34,35 @@
 
 
 def head_grad(q_raw, k_raw, values_in, out_grad, gain_q, gain_k):
-    q_full = q_raw.astype(jnp.float32)
-    k_full = k_raw.astype(jnp.float32)
-    inv_q = lax.rsqrt(jnp.mean(q_full * q_full, -1, keepdims=True) + EPSILON)
-    inv_k = lax.rsqrt(jnp.mean(k_full * k_full, -1, keepdims=True) + EPSILON)
-    unit_q = q_full * inv_q
-    unit_k = k_full * inv_k
-    q_norm = (unit_q * gain_q).astype(jnp.bfloat16)
-    k_norm = (unit_k * gain_k).astype(jnp.bfloat16)
+    def normed(raw, gain):
+        full = raw.astype(jnp.float32)
+        inverse = lax.rsqrt(jnp.mean(full * full, -1, keepdims=True) + EPSILON)
+        unit = full * inverse
+        return unit, inverse, (unit * gain).astype(jnp.bfloat16)
+
+    unit_q, inv_q, q_norm = normed(q_raw, gain_q)
+    unit_k, inv_k, k_norm = normed(k_raw, gain_k)
+    yield
     scores = matmul(k_norm, q_norm, NT)
     prob_grad = matmul(values_in, out_grad, NT)
-    top = jnp.max(scores, 0, keepdims=True)
-    probs = jnp.exp2((scores - top) * EXP2_SCALE)
-    probs = probs * (1.0 / jnp.sum(probs, 0, keepdims=True))
-    delta = jnp.sum(probs * prob_grad, 0, keepdims=True)
-    score_grad = (probs * (prob_grad - delta)).astype(jnp.bfloat16)
-    value_grad = matmul(probs.astype(jnp.bfloat16), out_grad, NN).astype(jnp.bfloat16)
+    yield
+    probs_parts, score_grad_parts = [], []
+    for first in range(0, TOKENS, PART):
+        part = scores[:, first : first + PART]
+        grad_part = prob_grad[:, first : first + PART]
+        top = jnp.max(part, 0, keepdims=True)
+        probs = jnp.exp2((part - top) * EXP2_SCALE)
+        probs = probs * (1.0 / jnp.sum(probs, 0, keepdims=True))
+        delta = jnp.sum(probs * grad_part, 0, keepdims=True)
+        probs_parts.append(probs.astype(jnp.bfloat16))
+        score_grad_parts.append((probs * (grad_part - delta)).astype(jnp.bfloat16))
+        yield
+    probs_low = jnp.concatenate(probs_parts, 1)
+    score_grad = jnp.concatenate(score_grad_parts, 1)
+    value_grad = matmul(probs_low, out_grad, NN).astype(jnp.bfloat16)
     kn_grad = matmul(score_grad, q_norm, NN)
     qn_grad = matmul(score_grad, k_norm, TN)
+    yield
 
     def raw_grad(norm_grad, unit, inverse, gain):
         along = norm_grad * unit
@@ -60,9 +72,25 @@
         raw = inverse * (norm_grad * scaled_gain - unit * mean)
         return raw.astype(jnp.bfloat16), gain_grad
 
+    k_grad, gain_k_grad = raw_grad(kn_grad, unit_k, inv_k, gain_k)
+    yield
     q_grad, gain_q_grad = raw_grad(qn_grad, unit_q, inv_q, gain_q)
-    k_grad, gain_k_grad = raw_grad(kn_grad, unit_k, inv_k, gain_k)
     return (q_grad, k_grad, value_grad), gain_q_grad, gain_k_grad
+
+
+def side_by_side(heads):
+    results = [None] * len(heads)
+    left, turn = set(range(len(heads))), 0
+    while left:
+        for index in sorted(left):
+            if index <= turn:
+                try:
+                    next(heads[index])
+                except StopIteration as end:
+                    results[index] = end.value
+                    left.discard(index)
+        turn += 1
+    return results
 
 
 def each(count, body):
@@ -183,15 +211,28 @@
     gains_copy.wait()
     each(4, lambda a: load(a).wait())
 
-    def compute(operands, block, head):
-        results, gain_q_grad, gain_k_grad = head_grad(
-            *(x.reshape(TOKENS, HD) for x in operands),
-            gains[block, head, 0:1, :],
-            gains[block, head, 1:2, :],
-        )
-        sums[block * HEADS + head, 0:1, :] = gain_q_grad
-        sums[block * HEADS + head, 1:2, :] = gain_k_grad
-        return results
+    def operands(block, u):
+        if block == 0:
+            return [x0[a, :, :, :, features(u)].reshape(TOKENS, HD) for a in range(4)]
+        return [x1[u, a].reshape(TOKENS, HD) for a in range(4)]
+
+    def compute(pair):
+        heads = [u if block == 0 else unit(u)[2] for block, u in pair]
+        running = [
+            head_grad(*operands(block, u), gains[block, head, 0:1, :], gains[block, head, 1:2, :])
+            for (block, u), head in zip(pair, heads)
+        ]
+        for (block, u), head, result in zip(pair, heads, side_by_side(running)):
+            results, gain_q_grad, gain_k_grad = result
+            sums[block * HEADS + head, 0:1, :] = gain_q_grad
+            sums[block * HEADS + head, 1:2, :] = gain_k_grad
+            for a in range(3):
+                if block == 0:
+                    grads[0, a, :, :, :, features(u)] = results[a].reshape(WT, WH, WW, HD)
+                else:
+                    quads = results[a].reshape(4, HALF_H, WW, HD)
+                    w1[u, a] = quads[1:]
+                    grads[(1, a) + quadrant(u, 0)] = quads[0]
 
     def start_outputs(u):
         for slot in (2, 3, 1):
@@ -204,24 +245,29 @@
     edge = lax.rem(t, min(n_t, GROUP))
     held = jnp.logical_or(edge == 0, edge == min(n_t, GROUP) - 1)
 
-    def step(u):
-        results = compute([x0[a, :, :, :, features(u)] for a in range(4)], 0, u)
-        for a in range(3):
-            grads[0, a, :, :, :, features(u)] = results[a].reshape(WT, WH, WW, HD)
+    def wait_inputs(u):
         in_local(u).wait()
         for slot in (1, 2, 3):
             in_copy(u, slot).wait_recv()
-        results = compute([x1[u, a] for a in range(4)], 1, unit(u)[2])
-        for a in range(3):
-            quads = results[a].reshape(4, HALF_H, WW, HD)
-            w1[u, a] = quads[1:]
-            grads[(1, a) + quadrant(u, 0)] = quads[0]
+
+    def step(u):
+        wait_inputs(u)
+        compute([(0, u + 2), (1, u)])
 
         @pl.when(jnp.logical_not(held))
         def _():
             start_outputs(u)
 
-    each(HEADS, step)
+    compute([(0, 0), (0, 1)])
+    each(HEADS - 2, step)
+    wait_inputs(HEADS - 2)
+    wait_inputs(HEADS - 1)
+    compute([(1, HEADS - 2), (1, HEADS - 1)])
+
+    @pl.when(jnp.logical_not(held))
+    def _():
+        start_outputs(HEADS - 2)
+        start_outputs(HEADS - 1)
 
     size = 2 * HEADS // near_h
 
@@ -257,15 +303,10 @@
 
         @pl.when(held)
         def _():
-            def send(i):
-                u = stage * batch + i
+            for u in range(stage * batch, (stage + 1) * batch):
                 start_outputs(u)
-
-                @pl.when(u > 0)
-                def _():
+                if u > 0:
                     wait_outputs(u - 1)
-
-            each(batch, send)
 
         for k in range(1, count):
             sum_copy(stage, k).wait_recv()

time: 67.2 us -> 65.9 us (0.981)
  the two profiles are of different devices: /device:TPU:1 before, /device:TPU:5 now
where the time goes in v6:
time: 65.9 us; the launch traced here: 65.8 us
  Pallas kernels  62.4 us (95%)
  local copies, waits for them, and re-layouts  2.8 us (4%)
    pallas_call x1, Pallas kernels, shards(): pl.pallas_call(functools.partial(grad_kernel, n_t, n_h), out_shape=(pltpu...  62.4 us
    unnamed x2, local copies, waits for them, and re-layouts  2.8 us

profile of v6, /device:TPU:5, one launch (start us, length us, event | category | flops | bytes accessed | tf_op | source)
XLA Modules:
  0.0 65.8 jit_solution(12371082356225443349)
XLA Ops:
  0.6 62.4 %shard_map.41 = (bf16[2,3,2,8,16,1536]{5,4,3,2,1,0:T(8,128)(2,1)S(1)}, f32[2,12,2,128]{3,2,1,0:T(2,128)S(1)}) custom-call(bf16[2,4,2,8,16,1536]{5,4,3,2,1,0:T(8,128)(2,1)} %saved.1, f32[2,12,2,128]{3,2,1,0:T(2,128)} %bitcast.3), custom_call_target="tpu_custom_call" | custom-call | tf_op jit(solution)/shard_map/pallas_call | solution.py:344
  63.0 2.2 %copy.6 = bf16[2,3,2,8,16,1536]{5,4,3,2,1,0:T(8,128)(2,1)} copy(bf16[2,3,2,8,16,1536]{5,4,3,2,1,0:T(8,128)(2,1)S(1)} %get-tuple-element.6) | data formatting | bytes 9437184
  65.2 0.6 copy.7

commit v7 on v6

--- a/solution.py
+++ b/solution.py
@@ -242,9 +242,6 @@
         for slot in (2, 3, 1):
             out_copy(u, slot).wait_send()
 
-    edge = lax.rem(t, min(n_t, GROUP))
-    held = jnp.logical_or(edge == 0, edge == min(n_t, GROUP) - 1)
-
     def wait_inputs(u):
         in_local(u).wait()
         for slot in (1, 2, 3):
@@ -253,21 +250,12 @@
     def step(u):
         wait_inputs(u)
         compute([(0, u + 2), (1, u)])
-
-        @pl.when(jnp.logical_not(held))
-        def _():
-            start_outputs(u)
 
     compute([(0, 0), (0, 1)])
     each(HEADS - 2, step)
     wait_inputs(HEADS - 2)
     wait_inputs(HEADS - 1)
     compute([(1, HEADS - 2), (1, HEADS - 1)])
-
-    @pl.when(jnp.logical_not(held))
-    def _():
-        start_outputs(HEADS - 2)
-        start_outputs(HEADS - 1)
 
     size = 2 * HEADS // near_h
 
@@ -300,14 +288,10 @@
             totals[here] = value
         for k in range(1, count):
             sum_copy(stage, k).start()
-
-        @pl.when(held)
-        def _():
-            for u in range(stage * batch, (stage + 1) * batch):
-                start_outputs(u)
-                if u > 0:
-                    wait_outputs(u - 1)
-
+        for u in range(stage * batch, (stage + 1) * batch):
+            start_outputs(u)
+            if u > 0:
+                wait_outputs(u - 1)
         for k in range(1, count):
             sum_copy(stage, k).wait_recv()
         if stage < 3:
@@ -322,10 +306,7 @@
             in_copy(u, slot).wait_send()
             out_copy(u, slot).wait_recv()
 
-        @pl.when(jnp.logical_or(jnp.logical_not(held), u == HEADS - 1))
-        def _():
-            wait_outputs(u)
-
+    wait_outputs(HEADS - 1)
     each(HEADS, finish)
 
 

time: 65.9 us -> 68.8 us (1.044)
  Pallas kernels: 62.4 us -> 65.3 us
    pallas_call x1, Pallas kernels: 62.4 us -> 65.3 us  [shards(): pl.pallas_call(functools.partial(grad_kernel, n_t, n_h), out_shape=(pltpu...]
where the time goes in v7:
time: 68.8 us; the launch traced here: 68.7 us
  Pallas kernels  65.3 us (95%)
  local copies, waits for them, and re-layouts  2.8 us (4%)
    pallas_call x1, Pallas kernels, shards(): pl.pallas_call(functools.partial(grad_kernel, n_t, n_h), out_shape=(pltpu...  65.3 us
    unnamed x2, local copies, waits for them, and re-layouts  2.8 us

profile of v7, /device:TPU:5, one launch (start us, length us, event | category | flops | bytes accessed | tf_op | source)
XLA Modules:
  0.0 68.7 jit_solution(15965615359139737458)
XLA Ops:
  0.6 65.3 %shard_map.41 = (bf16[2,3,2,8,16,1536]{5,4,3,2,1,0:T(8,128)(2,1)S(1)}, f32[2,12,2,128]{3,2,1,0:T(2,128)S(1)}) custom-call(bf16[2,4,2,8,16,1536]{5,4,3,2,1,0:T(8,128)(2,1)} %saved.1, f32[2,12,2,128]{3,2,1,0:T(2,128)} %bitcast.3), custom_call_target="tpu_custom_call" | custom-call | tf_op jit(solution)/shard_map/pallas_call | solution.py:325
  65.9 2.2 %copy.6 = bf16[2,3,2,8,16,1536]{5,4,3,2,1,0:T(8,128)(2,1)} copy(bf16[2,3,2,8,16,1536]{5,4,3,2,1,0:T(8,128)(2,1)S(1)} %get-tuple-element.6) | data formatting | bytes 9437184
  68.1 0.6 copy.7

commit v8 on v7

--- a/solution.py
+++ b/solution.py
@@ -33,15 +33,26 @@
     return lax.dot_general(a, b, dims, preferred_element_type=jnp.float32)
 
 
+def feature_means(*arrays):
+    full = jnp.concatenate(arrays, 0)
+    high = full.astype(jnp.bfloat16)
+    low = (full - high.astype(jnp.float32)).astype(jnp.bfloat16)
+    weights = jnp.full((2 * HD, HD), 1.0 / HD, jnp.bfloat16)
+    means = matmul(jnp.concatenate([high, low], 1), weights, NN)
+    return [means[i * TOKENS : (i + 1) * TOKENS] for i in range(len(arrays))]
+
+
 def head_grad(q_raw, k_raw, values_in, out_grad, gain_q, gain_k):
-    def normed(raw, gain):
-        full = raw.astype(jnp.float32)
-        inverse = lax.rsqrt(jnp.mean(full * full, -1, keepdims=True) + EPSILON)
-        unit = full * inverse
-        return unit, inverse, (unit * gain).astype(jnp.bfloat16)
-
-    unit_q, inv_q, q_norm = normed(q_raw, gain_q)
-    unit_k, inv_k, k_norm = normed(k_raw, gain_k)
+    q_full = q_raw.astype(jnp.float32)
+    k_full = k_raw.astype(jnp.float32)
+    square_q, square_k = feature_means(q_full * q_full, k_full * k_full)
+    yield
+    inv_q = lax.rsqrt(square_q + EPSILON)
+    inv_k = lax.rsqrt(square_k + EPSILON)
+    unit_q = q_full * inv_q
+    unit_k = k_full * inv_k
+    q_norm = (unit_q * gain_q).astype(jnp.bfloat16)
+    k_norm = (unit_k * gain_k).astype(jnp.bfloat16)
     yield
     scores = matmul(k_norm, q_norm, NT)
     prob_grad = matmul(values_in, out_grad, NT)
@@ -64,17 +75,16 @@
     qn_grad = matmul(score_grad, k_norm, TN)
     yield
 
-    def raw_grad(norm_grad, unit, inverse, gain):
-        along = norm_grad * unit
-        gain_grad = jnp.sum(along, 0, keepdims=True) * SCALE
-        scaled_gain = gain * SCALE
-        mean = jnp.mean(along * scaled_gain, -1, keepdims=True)
-        raw = inverse * (norm_grad * scaled_gain - unit * mean)
-        return raw.astype(jnp.bfloat16), gain_grad
-
-    k_grad, gain_k_grad = raw_grad(kn_grad, unit_k, inv_k, gain_k)
-    yield
-    q_grad, gain_q_grad = raw_grad(qn_grad, unit_q, inv_q, gain_q)
+    along_q = qn_grad * unit_q
+    along_k = kn_grad * unit_k
+    gain_q_grad = jnp.sum(along_q, 0, keepdims=True) * SCALE
+    gain_k_grad = jnp.sum(along_k, 0, keepdims=True) * SCALE
+    scaled_q = gain_q * SCALE
+    scaled_k = gain_k * SCALE
+    mean_q, mean_k = feature_means(along_q * scaled_q, along_k * scaled_k)
+    yield
+    q_grad = (inv_q * (qn_grad * scaled_q - unit_q * mean_q)).astype(jnp.bfloat16)
+    k_grad = (inv_k * (kn_grad * scaled_k - unit_k * mean_k)).astype(jnp.bfloat16)
     return (q_grad, k_grad, value_grad), gain_q_grad, gain_k_grad
 
 
@@ -238,10 +248,6 @@
         for slot in (2, 3, 1):
             out_copy(u, slot).start()
 
-    def wait_outputs(u):
-        for slot in (2, 3, 1):
-            out_copy(u, slot).wait_send()
-
     def wait_inputs(u):
         in_local(u).wait()
         for slot in (1, 2, 3):
@@ -250,12 +256,15 @@
     def step(u):
         wait_inputs(u)
         compute([(0, u + 2), (1, u)])
+        start_outputs(u)
 
     compute([(0, 0), (0, 1)])
     each(HEADS - 2, step)
     wait_inputs(HEADS - 2)
     wait_inputs(HEADS - 1)
     compute([(1, HEADS - 2), (1, HEADS - 1)])
+    start_outputs(HEADS - 2)
+    start_outputs(HEADS - 1)
 
     size = 2 * HEADS // near_h
 
@@ -279,7 +288,6 @@
 
     here = pl.ds(place(0) * size, size)
     value = sums[here]
-    batch = HEADS // 4
     for stage in range(4):
         count = counts[stage]
         if stage < 3:
@@ -288,10 +296,6 @@
             totals[here] = value
         for k in range(1, count):
             sum_copy(stage, k).start()
-        for u in range(stage * batch, (stage + 1) * batch):
-            start_outputs(u)
-            if u > 0:
-                wait_outputs(u - 1)
         for k in range(1, count):
             sum_copy(stage, k).wait_recv()
         if stage < 3:
@@ -304,9 +308,8 @@
     def finish(u):
         for slot in (1, 2, 3):
             in_copy(u, slot).wait_send()
-            out_copy(u, slot).wait_recv()
-
-    wait_outputs(HEADS - 1)
+            out_copy(u, slot).wait()
+
     each(HEADS, finish)
 
 

time: 68.8 us -> 62.1 us (0.903)
  the two profiles are of different devices: /device:TPU:5 before, /device:TPU:1 now
where the time goes in v8:
time: 62.1 us; the launch traced here: 62 us
  Pallas kernels  58.6 us (94%)
  local copies, waits for them, and re-layouts  2.8 us (5%)
  between operations  0.64 us (1%)
    pallas_call x1, Pallas kernels, shards(): pl.pallas_call(functools.partial(grad_kernel, n_t, n_h), out_shape=(pltpu...  58.6 us
    unnamed x2, local copies, waits for them, and re-layouts  2.8 us

profile of v8, /device:TPU:1, one launch (start us, length us, event | category | flops | bytes accessed | tf_op | source)
XLA Modules:
  0.0 62.0 jit_solution(13704341357492948038)
XLA Ops:
  0.6 58.6 %shard_map.41 = (bf16[2,3,2,8,16,1536]{5,4,3,2,1,0:T(8,128)(2,1)S(1)}, f32[2,12,2,128]{3,2,1,0:T(2,128)S(1)}) custom-call(bf16[2,4,2,8,16,1536]{5,4,3,2,1,0:T(8,128)(2,1)} %saved.1, f32[2,12,2,128]{3,2,1,0:T(2,128)} %bitcast.3), custom_call_target="tpu_custom_call" | custom-call | tf_op jit(solution)/shard_map/pallas_call | solution.py:328
  59.2 2.2 %copy.6 = bf16[2,3,2,8,16,1536]{5,4,3,2,1,0:T(8,128)(2,1)} copy(bf16[2,3,2,8,16,1536]{5,4,3,2,1,0:T(8,128)(2,1)S(1)} %get-tuple-element.6) | data formatting | bytes 9437184
  61.4 0.6 copy.7

commit v9 on v8

--- a/solution.py
+++ b/solution.py
@@ -17,6 +17,7 @@
 TOKENS = WT * WH * WW
 PART = 128
 ROLES = 4
+SHARE = HEADS // ROLES
 GROUP = 8
 
 EPSILON = 1e-06
@@ -115,6 +116,8 @@
 ):
     t = lax.axis_index("tm")
     h = lax.axis_index("height")
+    near_h, near_t = min(n_h, GROUP), min(n_t, GROUP)
+    far_h, far_t = n_h // near_h, n_t // near_t
 
     def at(dt, dh):
         return (lax.rem(t + dt + n_t, n_t), lax.rem(h + dh + n_h, n_h))
@@ -122,9 +125,19 @@
     def features(head):
         return pl.ds(pl.multiple_of(head * HD, HD), HD)
 
+    in_t, in_h = lax.rem(t, near_t), lax.rem(h, near_h)
+    across = jnp.logical_and(near_t >= 4, jnp.logical_or(in_h == 0, in_h == near_h - 1))
+    outer = jnp.logical_and(across, jnp.logical_or(in_t == 0, in_t == near_t - 1))
+    inner = jnp.logical_and(across, jnp.logical_or(in_t == 1, in_t == near_t - 2))
+    own_a = jnp.where(jnp.logical_or(in_t == 1, in_t == near_t - 1), 1, 0)
+    own_b = jnp.where(in_h == 0, 1, 0)
+    side = jnp.where(outer, 1 - own_a, own_a)
+
     def unit(u):
-        role = lax.rem(u, ROLES)
-        return lax.rem(role, 2), role // 2, role * (HEADS // ROLES) + u // ROLES
+        taken = u >= HEADS
+        role = jnp.where(taken, side + 2 * own_b, lax.rem(u, ROLES))
+        first = jnp.where(taken, (1 - side + 2 * own_b) * SHARE - HEADS, role * SHARE)
+        return lax.rem(role, 2), role // 2, first + jnp.where(taken, u, u // ROLES)
 
     def holder(u, slot):
         rt, rh, _ = unit(u)
@@ -133,6 +146,12 @@
     def quadrant(u, slot):
         a, b = holder(u, slot)
         return 1 - a, pl.ds((1 - b) * HALF_H, HALF_H), slice(None), features(unit(u)[2])
+
+    def regular(u, slot):
+        (rt, _, _), (a, b) = unit(u), holder(u, slot)
+        here = jnp.logical_and(a == own_a, b == own_b)
+        moved = jnp.logical_and(jnp.logical_or(outer, inner), rt != side)
+        return jnp.logical_not(jnp.logical_and(here, moved))
 
     def owner(u, slot):
         (rt, rh, _), (a, b) = unit(u), holder(u, slot)
@@ -152,6 +171,19 @@
             device_id_type=MESH,
         )
 
+    def taken_copy(j, slot):
+        rh = own_b if slot % 2 == 0 else 1 - own_b
+        head = (1 - side + 2 * rh) * SHARE + j
+        band = pl.ds((1 - own_b) * HALF_H, HALF_H)
+        return pltpu.make_async_remote_copy(
+            src_ref=saved.at[1, :, 1 - own_a, band, :, features(head)],
+            dst_ref=x1.at[HEADS + j, :, slot],
+            send_sem=in_send.at[HEADS + j, slot - 1],
+            recv_sem=in_recv.at[HEADS + j, slot - 1],
+            device_id=at(side - own_a, rh - own_b),
+            device_id_type=MESH,
+        )
+
     def in_local(u):
         return pltpu.make_async_copy(
             saved.at[(1, slice(None)) + quadrant(u, 0)], x1.at[u, :, 0], load1.at[u]
@@ -170,8 +202,6 @@
     def load(a):
         return pltpu.make_async_copy(saved.at[0, a], x0.at[a], load0.at[a])
 
-    near_h, near_t = min(n_h, GROUP), min(n_t, GROUP)
-    far_h, far_t = n_h // near_h, n_t // near_t
     counts = (near_h, far_h * far_t, near_t, near_h)
 
     def place(stage):
@@ -191,11 +221,6 @@
         shift = other - place(stage)
         return other, ((t + shift, h) if stage == 2 else (t, h + shift))
 
-    gains_copy = pltpu.make_async_copy(gains_far, gains, load_gains)
-    gains_copy.start()
-    each(4, lambda a: load(a).start())
-    each(HEADS, lambda u: in_local(u).start())
-
     barrier = pltpu.get_barrier_semaphore()
 
     def greet(device):
@@ -211,13 +236,24 @@
         for k in range(1, counts[stage]):
             greet(peer(stage, k)[1])
             greeted += 1
+    gains_copy = pltpu.make_async_copy(gains_far, gains, load_gains)
+    gains_copy.start()
+    each(4, lambda a: load(a).start())
+    each(HEADS, lambda u: pl.when(regular(u, 0))(lambda: in_local(u).start()))
+    pl.when(inner)(lambda: each(SHARE, lambda j: in_local(HEADS + j).start()))
     pl.semaphore_wait(barrier, greeted)
 
     def start_inputs(u):
         for slot in (2, 3, 1):
-            in_copy(u, slot).start()
+            pl.when(regular(u, slot))(in_copy(u, slot).start)
+
+    def start_taken(j):
+        pl.when(outer)(taken_copy(j, 2).start)
+        pl.when(outer)(taken_copy(j, 3).start)
+        pl.when(inner)(taken_copy(j, 1).start)
 
     each(HEADS, start_inputs)
+    each(SHARE, start_taken)
     gains_copy.wait()
     each(4, lambda a: load(a).wait())
 
@@ -226,16 +262,23 @@
             return [x0[a, :, :, :, features(u)].reshape(TOKENS, HD) for a in range(4)]
         return [x1[u, a].reshape(TOKENS, HD) for a in range(4)]
 
-    def compute(pair):
+    def compute(pair, twice=False):
         heads = [u if block == 0 else unit(u)[2] for block, u in pair]
         running = [
             head_grad(*operands(block, u), gains[block, head, 0:1, :], gains[block, head, 1:2, :])
             for (block, u), head in zip(pair, heads)
         ]
-        for (block, u), head, result in zip(pair, heads, side_by_side(running)):
+        for index, result in enumerate(side_by_side(running)):
+            (block, u), head = pair[index], heads[index]
             results, gain_q_grad, gain_k_grad = result
-            sums[block * HEADS + head, 0:1, :] = gain_q_grad
-            sums[block * HEADS + head, 1:2, :] = gain_k_grad
+            for i, gain_grad in enumerate((gain_q_grad, gain_k_grad)):
+                row = (block * HEADS + head, slice(i, i + 1))
+                if block == 0:
+                    sums[row] = gain_grad
+                elif index == 0:
+                    sums[row] += gain_grad
+                else:
+                    sums[row] += jnp.where(twice, 0.0, gain_grad)
             for a in range(3):
                 if block == 0:
                     grads[0, a, :, :, :, features(u)] = results[a].reshape(WT, WH, WW, HD)
@@ -253,18 +296,35 @@
         for slot in (1, 2, 3):
             in_copy(u, slot).wait_recv()
 
-    def step(u):
+    def listed(position):
+        role = lax.rem(position, ROLES - 1)
+        role = role + jnp.where(role >= own_a + 2 * own_b, 1, 0)
+        return jnp.where(outer, position // (ROLES - 1) * ROLES + role, position)
+
+    ahead = jnp.where(outer, 2, 1)
+
+    def still_pair(i):
+        compute([(0, 2 * i), (0, 2 * i + 1)])
+
+    def mixed_pair(i):
+        u = listed(i)
         wait_inputs(u)
-        compute([(0, u + 2), (1, u)])
+        compute([(0, jnp.minimum(i + 2 * ahead, HEADS - 1)), (1, u)])
         start_outputs(u)
 
-    compute([(0, 0), (0, 1)])
-    each(HEADS - 2, step)
-    wait_inputs(HEADS - 2)
-    wait_inputs(HEADS - 1)
-    compute([(1, HEADS - 2), (1, HEADS - 1)])
-    start_outputs(HEADS - 2)
-    start_outputs(HEADS - 1)
+    def shifted_pair(i):
+        u = HEADS - 2 + 2 * i
+        v = jnp.minimum(u + 1, HEADS + SHARE - 1)
+        wait_inputs(u)
+        pl.when(u != v)(lambda: wait_inputs(v))
+        compute([(1, u), (1, v)], u == v)
+        start_outputs(u)
+        pl.when(u != v)(lambda: start_outputs(v))
+
+    sums[...] = jnp.zeros_like(sums)
+    each(ahead, still_pair)
+    each(jnp.where(outer, HEADS - SHARE, HEADS - 2), mixed_pair)
+    each(jnp.where(outer, 0, jnp.where(inner, 3, 1)), shifted_pair)
 
     size = 2 * HEADS // near_h
 
@@ -307,10 +367,19 @@
 
     def finish(u):
         for slot in (1, 2, 3):
-            in_copy(u, slot).wait_send()
-            out_copy(u, slot).wait()
+            pl.when(regular(u, slot))(in_copy(u, slot).wait_send)
+            pl.when(regular(u, slot))(out_copy(u, slot).wait_recv)
+            pl.when(regular(u, 0))(out_copy(u, slot).wait_send)
+
+    def finish_taken(j):
+        for slot in (1, 2, 3):
+            holds = inner if slot == 1 else outer
+            pl.when(holds)(taken_copy(j, slot).wait_send)
+            pl.when(holds)(out_copy(HEADS + j, slot).wait_recv)
+            pl.when(inner)(out_copy(HEADS + j, slot).wait_send)
 
     each(HEADS, finish)
+    each(SHARE, finish_taken)
 
 
 def solution(mesh):
@@ -332,19 +401,19 @@
             out_specs=(near, near),
             scratch_shapes=[
                 pltpu.VMEM(saved.shape[1:], jnp.bfloat16),
-                pltpu.VMEM((HEADS, 4) + quads, jnp.bfloat16),
-                pltpu.VMEM((HEADS, 3, 3) + quads[1:], jnp.bfloat16),
+                pltpu.VMEM((HEADS + SHARE, 4) + quads, jnp.bfloat16),
+                pltpu.VMEM((HEADS + SHARE, 3, 3) + quads[1:], jnp.bfloat16),
                 pltpu.VMEM((2, HEADS, 2, HD), jnp.float32),
                 pltpu.VMEM((2 * HEADS, 2, HD), jnp.float32),
                 pltpu.VMEM((3, GROUP, 2 * HEADS // min(n_h, GROUP), 2, HD), jnp.float32),
                 pltpu.VMEM((2 * HEADS, 2, HD), jnp.float32),
                 dma,
                 dma((4,)),
-                dma((HEADS,)),
-                dma((HEADS, 3)),
-                dma((HEADS, 3)),
-                dma((HEADS, 3)),
-                dma((HEADS, 3)),
+                dma((HEADS + SHARE,)),
+                dma((HEADS + SHARE, 3)),
+                dma((HEADS + SHARE, 3)),
+                dma((HEADS + SHARE, 3)),
+                dma((HEADS + SHARE, 3)),
                 dma((4, GROUP)),
                 dma((4, GROUP)),
             ],

time: 62.1 us -> 61.5 us (level)
  no operation moved by 1% of the time
where the time goes in v9:
time: 61.5 us; the launch traced here: 61.4 us
  Pallas kernels  58 us (94%)
  local copies, waits for them, and re-layouts  2.8 us (5%)
  between operations  0.64 us (1%)
    pallas_call x1, Pallas kernels, shards(): pl.pallas_call(functools.partial(grad_kernel, n_t, n_h), out_shape=(pltpu...  58 us
    unnamed x2, local copies, waits for them, and re-layouts  2.8 us

profile of v9, /device:TPU:1, one launch (start us, length us, event | category | flops | bytes accessed | tf_op | source)
XLA Modules:
  0.0 61.4 jit_solution(1203481371436708735)
XLA Ops:
  0.6 58.0 %shard_map.41 = (bf16[2,3,2,8,16,1536]{5,4,3,2,1,0:T(8,128)(2,1)S(1)}, f32[2,12,2,128]{3,2,1,0:T(2,128)S(1)}) custom-call(bf16[2,4,2,8,16,1536]{5,4,3,2,1,0:T(8,128)(2,1)} %saved.1, f32[2,12,2,128]{3,2,1,0:T(2,128)} %bitcast.3), custom_call_target="tpu_custom_call" | custom-call | tf_op jit(solution)/shard_map/pallas_call | solution.py:397
  58.6 2.2 %copy.6 = bf16[2,3,2,8,16,1536]{5,4,3,2,1,0:T(8,128)(2,1)} copy(bf16[2,3,2,8,16,1536]{5,4,3,2,1,0:T(8,128)(2,1)S(1)} %get-tuple-element.6) | data formatting | bytes 9437184
  60.8 0.6 copy.7

commit v10 on v7

--- a/solution.py
+++ b/solution.py
@@ -16,6 +16,7 @@
 HALF_H = WH // 2
 TOKENS = WT * WH * WW
 PART = 128
+ROWS = 64
 ROLES = 4
 GROUP = 8
 
@@ -33,12 +34,28 @@
     return lax.dot_general(a, b, dims, preferred_element_type=jnp.float32)
 
 
+def rows_of(array, first):
+    return array[first : first + ROWS]
+
+
+def column_sum(blocks):
+    tiles = [block.reshape(-1, 8, block.shape[-1]).sum(0) for block in blocks]
+    return jnp.sum(functools.reduce(jnp.add, tiles), 0, keepdims=True)
+
+
 def head_grad(q_raw, k_raw, values_in, out_grad, gain_q, gain_k):
+    blocks = range(0, TOKENS, ROWS)
+
     def normed(raw, gain):
-        full = raw.astype(jnp.float32)
-        inverse = lax.rsqrt(jnp.mean(full * full, -1, keepdims=True) + EPSILON)
-        unit = full * inverse
-        return unit, inverse, (unit * gain).astype(jnp.bfloat16)
+        units, inverses, norms = [], [], []
+        for first in blocks:
+            full = rows_of(raw, first).astype(jnp.float32)
+            inverse = lax.rsqrt(jnp.mean(full * full, -1, keepdims=True) + EPSILON)
+            unit = full * inverse
+            units.append(unit)
+            inverses.append(inverse)
+            norms.append((unit * gain).astype(jnp.bfloat16))
+        return units, inverses, jnp.concatenate(norms, 0)
 
     unit_q, inv_q, q_norm = normed(q_raw, gain_q)
     unit_k, inv_k, k_norm = normed(k_raw, gain_k)
@@ -46,31 +63,46 @@
     scores = matmul(k_norm, q_norm, NT)
     prob_grad = matmul(values_in, out_grad, NT)
     yield
-    probs_parts, score_grad_parts = [], []
-    for first in range(0, TOKENS, PART):
-        part = scores[:, first : first + PART]
-        grad_part = prob_grad[:, first : first + PART]
+    low_parts, score_grad_parts = [], []
+    for first_query in range(0, TOKENS, PART):
+        part = scores[:, first_query : first_query + PART]
+        grad_part = prob_grad[:, first_query : first_query + PART]
         top = jnp.max(part, 0, keepdims=True)
-        probs = jnp.exp2((part - top) * EXP2_SCALE)
-        probs = probs * (1.0 / jnp.sum(probs, 0, keepdims=True))
-        delta = jnp.sum(probs * grad_part, 0, keepdims=True)
-        probs_parts.append(probs.astype(jnp.bfloat16))
-        score_grad_parts.append((probs * (grad_part - delta)).astype(jnp.bfloat16))
+        powers = [jnp.exp2((rows_of(part, first) - top) * EXP2_SCALE) for first in blocks]
+        inverse = 1.0 / column_sum(powers)
+        probs, weighted, low = [], [], []
+        for first, power in zip(blocks, powers):
+            probs.append(power * inverse)
+            weighted.append(probs[-1] * rows_of(grad_part, first))
+            low.append(probs[-1].astype(jnp.bfloat16))
+        delta = column_sum(weighted)
+        score_grad_parts.append(
+            jnp.concatenate(
+                [
+                    (prob * (rows_of(grad_part, first) - delta)).astype(jnp.bfloat16)
+                    for first, prob in zip(blocks, probs)
+                ],
+                0,
+            )
+        )
+        low_parts.append(jnp.concatenate(low, 0))
         yield
-    probs_low = jnp.concatenate(probs_parts, 1)
     score_grad = jnp.concatenate(score_grad_parts, 1)
-    value_grad = matmul(probs_low, out_grad, NN).astype(jnp.bfloat16)
+    value_grad = matmul(jnp.concatenate(low_parts, 1), out_grad, NN).astype(jnp.bfloat16)
     kn_grad = matmul(score_grad, q_norm, NN)
     qn_grad = matmul(score_grad, k_norm, TN)
     yield
 
-    def raw_grad(norm_grad, unit, inverse, gain):
-        along = norm_grad * unit
-        gain_grad = jnp.sum(along, 0, keepdims=True) * SCALE
+    def raw_grad(norm_grad, units, inverses, gain):
         scaled_gain = gain * SCALE
-        mean = jnp.mean(along * scaled_gain, -1, keepdims=True)
-        raw = inverse * (norm_grad * scaled_gain - unit * mean)
-        return raw.astype(jnp.bfloat16), gain_grad
+        alongs, raws = [], []
+        for first, unit, inverse in zip(blocks, units, inverses):
+            grad = rows_of(norm_grad, first)
+            along = grad * unit
+            mean = jnp.mean(along * scaled_gain, -1, keepdims=True)
+            raws.append((inverse * (grad * scaled_gain - unit * mean)).astype(jnp.bfloat16))
+            alongs.append(along)
+        return jnp.concatenate(raws, 0), column_sum(alongs) * SCALE
 
     k_grad, gain_k_grad = raw_grad(kn_grad, unit_k, inv_k, gain_k)
     yield
@@ -181,11 +213,6 @@
         shift = other - place(stage)
         return other, ((t + shift, h) if stage == 2 else (t, h + shift))
 
-    gains_copy = pltpu.make_async_copy(gains_far, gains, load_gains)
-    gains_copy.start()
-    each(4, lambda a: load(a).start())
-    each(HEADS, lambda u: in_local(u).start())
-
     barrier = pltpu.get_barrier_semaphore()
 
     def greet(device):
@@ -201,6 +228,10 @@
         for k in range(1, counts[stage]):
             greet(peer(stage, k)[1])
             greeted += 1
+    gains_copy = pltpu.make_async_copy(gains_far, gains, load_gains)
+    gains_copy.start()
+    each(4, lambda a: load(a).start())
+    each(HEADS, lambda u: in_local(u).start())
     pl.semaphore_wait(barrier, greeted)
 
     def start_inputs(u):
@@ -238,10 +269,6 @@
         for slot in (2, 3, 1):
             out_copy(u, slot).start()
 
-    def wait_outputs(u):
-        for slot in (2, 3, 1):
-            out_copy(u, slot).wait_send()
-
     def wait_inputs(u):
         in_local(u).wait()
         for slot in (1, 2, 3):
@@ -257,6 +284,7 @@
     wait_inputs(HEADS - 1)
     compute([(1, HEADS - 2), (1, HEADS - 1)])
 
+    batch = HEADS // 4
     size = 2 * HEADS // near_h
 
     def sum_copy(stage, k):
@@ -279,7 +307,6 @@
 
     here = pl.ds(place(0) * size, size)
     value = sums[here]
-    batch = HEADS // 4
     for stage in range(4):
         count = counts[stage]
         if stage < 3:
@@ -288,10 +315,7 @@
             totals[here] = value
         for k in range(1, count):
             sum_copy(stage, k).start()
-        for u in range(stage * batch, (stage + 1) * batch):
-            start_outputs(u)
-            if u > 0:
-                wait_outputs(u - 1)
+        each(batch, lambda i: start_outputs(stage * batch + i))
         for k in range(1, count):
             sum_copy(stage, k).wait_recv()
         if stage < 3:
@@ -304,9 +328,8 @@
     def finish(u):
         for slot in (1, 2, 3):
             in_copy(u, slot).wait_send()
-            out_copy(u, slot).wait_recv()
-
-    wait_outputs(HEADS - 1)
+            out_copy(u, slot).wait()
+
     each(HEADS, finish)
 
 

time: 68.8 us -> 66.4 us (0.965)
  the two profiles are of different devices: /device:TPU:5 before, /device:TPU:15 now
where the time goes in v10:
time: 66.4 us; the launch traced here: 66.3 us
  Pallas kernels  62.9 us (95%)
  local copies, waits for them, and re-layouts  2.8 us (4%)
    pallas_call x1, Pallas kernels, shards(): pl.pallas_call(functools.partial(grad_kernel, n_t, n_h), out_shape=(pltpu...  62.9 us
    unnamed x2, local copies, waits for them, and re-layouts  2.8 us

profile of v10, /device:TPU:15, one launch (start us, length us, event | category | flops | bytes accessed | tf_op | source)
XLA Modules:
  0.0 66.3 jit_solution(4618634925407589068)
XLA Ops:
  0.6 62.9 %shard_map.41 = (bf16[2,3,2,8,16,1536]{5,4,3,2,1,0:T(8,128)(2,1)S(1)}, f32[2,12,2,128]{3,2,1,0:T(2,128)S(1)}) custom-call(bf16[2,4,2,8,16,1536]{5,4,3,2,1,0:T(8,128)(2,1)} %saved.1, f32[2,12,2,128]{3,2,1,0:T(2,128)} %bitcast.3), custom_call_target="tpu_custom_call" | custom-call | tf_op jit(solution)/shard_map/pallas_call | solution.py:348
  63.5 2.2 %copy.6 = bf16[2,3,2,8,16,1536]{5,4,3,2,1,0:T(8,128)(2,1)} copy(bf16[2,3,2,8,16,1536]{5,4,3,2,1,0:T(8,128)(2,1)S(1)} %get-tuple-element.6) | data formatting | bytes 9437184
  65.7 0.6 copy.7

commit v11 on v10

--- a/solution.py
+++ b/solution.py
@@ -277,6 +277,7 @@
     def step(u):
         wait_inputs(u)
         compute([(0, u + 2), (1, u)])
+        start_outputs(u)
 
     compute([(0, 0), (0, 1)])
     each(HEADS - 2, step)
@@ -284,7 +285,6 @@
     wait_inputs(HEADS - 1)
     compute([(1, HEADS - 2), (1, HEADS - 1)])
 
-    batch = HEADS // 4
     size = 2 * HEADS // near_h
 
     def sum_copy(stage, k):
@@ -313,9 +313,11 @@
             stages[stage, place(stage)] = value
         else:
             totals[here] = value
-        for k in range(1, count):
+        for k in sorted(range(1, count), key=lambda k: -min(k, count - k)):
             sum_copy(stage, k).start()
-        each(batch, lambda i: start_outputs(stage * batch + i))
+        if stage == 0:
+            start_outputs(HEADS - 2)
+            start_outputs(HEADS - 1)
         for k in range(1, count):
             sum_copy(stage, k).wait_recv()
         if stage < 3:

time: 66.4 us -> 59.6 us (0.90)
  the two profiles are of different devices: /device:TPU:15 before, /device:TPU:1 now
where the time goes in v11:
time: 59.6 us; the launch traced here: 59.5 us
  Pallas kernels  56.1 us (94%)
  local copies, waits for them, and re-layouts  2.8 us (5%)
  between operations  0.64 us (1%)
    pallas_call x1, Pallas kernels, shards(): pl.pallas_call(functools.partial(grad_kernel, n_t, n_h), out_shape=(pltpu...  56.1 us
    unnamed x2, local copies, waits for them, and re-layouts  2.8 us

profile of v11, /device:TPU:1, one launch (start us, length us, event | category | flops | bytes accessed | tf_op | source)
XLA Modules:
  0.0 59.5 jit_solution(7395148910097224314)
XLA Ops:
  0.6 56.1 %shard_map.41 = (bf16[2,3,2,8,16,1536]{5,4,3,2,1,0:T(8,128)(2,1)S(1)}, f32[2,12,2,128]{3,2,1,0:T(2,128)S(1)}) custom-call(bf16[2,4,2,8,16,1536]{5,4,3,2,1,0:T(8,128)(2,1)} %saved.1, f32[2,12,2,128]{3,2,1,0:T(2,128)} %bitcast.3), custom_call_target="tpu_custom_call" | custom-call | tf_op jit(solution)/shard_map/pallas_call | solution.py:350
  56.7 2.2 %copy.6 = bf16[2,3,2,8,16,1536]{5,4,3,2,1,0:T(8,128)(2,1)} copy(bf16[2,3,2,8,16,1536]{5,4,3,2,1,0:T(8,128)(2,1)S(1)} %get-tuple-element.6) | data formatting | bytes 9437184
  58.9 0.6 %copy.7 = f32[2,2,12,128]{3,1,2,0:T(2,128)} copy(f32[2,2,12,128]{3,1,2,0:T(2,128)S(1)} %bitcast.2) | data formatting | bytes 49152

commit v12 on v10

--- a/solution.py
+++ b/solution.py
@@ -19,6 +19,7 @@
 ROWS = 64
 ROLES = 4
 GROUP = 8
+LAST = 3
 
 EPSILON = 1e-06
 SCALE = HD ** (-0.5)
@@ -129,11 +130,15 @@
     lax.fori_loop(0, count, lambda i, carry: (body(i), carry)[1], 0)
 
 
+def farthest_first(count):
+    return sorted(range(1, count), key=lambda k: -min(k, count - k))
+
+
 def grad_kernel(
     n_t, n_h,
     saved, gains_far, grads, gain_grads,
     x0, x1, w1, gains, sums, stages, totals,
-    load_gains, load0, load1, in_send, in_recv, out_send, out_recv, sum_send, sum_recv,
+    load_gains, load0, in_send, in_recv, out_send, out_recv, sum_send, sum_recv,
 ):
     t = lax.axis_index("tm")
     h = lax.axis_index("height")
@@ -168,23 +173,23 @@
         return pltpu.make_async_remote_copy(
             src_ref=saved.at[(1, slice(None)) + quadrant(u, slot)],
             dst_ref=x1.at[u, :, slot],
-            send_sem=in_send.at[u, slot - 1],
-            recv_sem=in_recv.at[u, slot - 1],
+            send_sem=in_send,
+            recv_sem=in_recv.at[u],
             device_id=worker(u, slot),
             device_id_type=MESH,
         )
 
     def in_local(u):
         return pltpu.make_async_copy(
-            saved.at[(1, slice(None)) + quadrant(u, 0)], x1.at[u, :, 0], load1.at[u]
+            saved.at[(1, slice(None)) + quadrant(u, 0)], x1.at[u, :, 0], in_recv.at[u]
         )
 
     def out_copy(u, slot):
         return pltpu.make_async_remote_copy(
             src_ref=w1.at[u, :, slot - 1],
             dst_ref=grads.at[(1, slice(None)) + quadrant(u, slot)],
-            send_sem=out_send.at[u, slot - 1],
-            recv_sem=out_recv.at[u, slot - 1],
+            send_sem=out_send,
+            recv_sem=out_recv,
             device_id=owner(u, slot),
             device_id_type=MESH,
         )
@@ -219,15 +224,15 @@
         pl.semaphore_signal(barrier, inc=1, device_id=device, device_id_type=MESH)
 
     greeted = 0
+    for stage in (2, 1, 0):
+        for k in farthest_first(counts[stage]):
+            greet(peer(stage, k)[1])
+            greeted += 1
     for dt in (-1, 0, 1):
         for dh in (-1, 0, 1):
             if dt or dh:
                 greet(at(dt, dh))
                 greeted += 1
-    for stage in range(3):
-        for k in range(1, counts[stage]):
-            greet(peer(stage, k)[1])
-            greeted += 1
     gains_copy = pltpu.make_async_copy(gains_far, gains, load_gains)
     gains_copy.start()
     each(4, lambda a: load(a).start())
@@ -269,14 +274,16 @@
         for slot in (2, 3, 1):
             out_copy(u, slot).start()
 
+    def drain(semaphore, ref):
+        pltpu.make_async_copy(ref, ref, semaphore).wait()
+
     def wait_inputs(u):
-        in_local(u).wait()
-        for slot in (1, 2, 3):
-            in_copy(u, slot).wait_recv()
+        drain(in_recv.at[u], x1.at[u])
 
     def step(u):
         wait_inputs(u)
         compute([(0, u + 2), (1, u)])
+        pl.when(u < HEADS - LAST)(lambda: start_outputs(u))
 
     compute([(0, 0), (0, 1)])
     each(HEADS - 2, step)
@@ -284,7 +291,6 @@
     wait_inputs(HEADS - 1)
     compute([(1, HEADS - 2), (1, HEADS - 1)])
 
-    batch = HEADS // 4
     size = 2 * HEADS // near_h
 
     def sum_copy(stage, k):
@@ -313,9 +319,10 @@
             stages[stage, place(stage)] = value
         else:
             totals[here] = value
-        for k in range(1, count):
+        for k in farthest_first(count):
             sum_copy(stage, k).start()
-        each(batch, lambda i: start_outputs(stage * batch + i))
+        for u in {0: (HEADS - 3, HEADS - 2), 1: (HEADS - 1,)}.get(stage, ()):
+            start_outputs(u)
         for k in range(1, count):
             sum_copy(stage, k).wait_recv()
         if stage < 3:
@@ -325,12 +332,9 @@
         for k in range(1, counts[stage]):
             sum_copy(stage, k).wait_send()
 
-    def finish(u):
-        for slot in (1, 2, 3):
-            in_copy(u, slot).wait_send()
-            out_copy(u, slot).wait()
-
-    each(HEADS, finish)
+    drain(in_send, x1.at[pl.ds(0, HEADS * 3 // 4)])
+    drain(out_send, w1)
+    drain(out_recv, w1)
 
 
 def solution(mesh):
@@ -360,11 +364,10 @@
                 pltpu.VMEM((2 * HEADS, 2, HD), jnp.float32),
                 dma,
                 dma((4,)),
+                dma,
                 dma((HEADS,)),
-                dma((HEADS, 3)),
-                dma((HEADS, 3)),
-                dma((HEADS, 3)),
-                dma((HEADS, 3)),
+                dma,
+                dma,
                 dma((4, GROUP)),
                 dma((4, GROUP)),
             ],

time: 66.4 us -> 58.4 us (0.88)
  the two profiles are of different devices: /device:TPU:15 before, /device:TPU:1 now
where the time goes in v12:
time: 58.4 us; the launch traced here: 58.3 us
  Pallas kernels  54.9 us (94%)
  local copies, waits for them, and re-layouts  2.8 us (5%)
  between operations  0.64 us (1%)
    pallas_call x1, Pallas kernels, shards(): pl.pallas_call(functools.partial(grad_kernel, n_t, n_h), out_shape=(pltpu...  54.9 us
    unnamed x2, local copies, waits for them, and re-layouts  2.8 us

profile of v12, /device:TPU:1, one launch (start us, length us, event | category | flops | bytes accessed | tf_op | source)
XLA Modules:
  0.0 58.3 jit_solution(17321811645711762245)
XLA Ops:
  0.6 54.9 %shard_map.41 = (bf16[2,3,2,8,16,1536]{5,4,3,2,1,0:T(8,128)(2,1)S(1)}, f32[2,12,2,128]{3,2,1,0:T(2,128)S(1)}) custom-call(bf16[2,4,2,8,16,1536]{5,4,3,2,1,0:T(8,128)(2,1)} %saved.1, f32[2,12,2,128]{3,2,1,0:T(2,128)} %bitcast.3), custom_call_target="tpu_custom_call" | custom-call | tf_op jit(solution)/shard_map/pallas_call | solution.py:352
  55.5 2.2 %copy.6 = bf16[2,3,2,8,16,1536]{5,4,3,2,1,0:T(8,128)(2,1)} copy(bf16[2,3,2,8,16,1536]{5,4,3,2,1,0:T(8,128)(2,1)S(1)} %get-tuple-element.6) | data formatting | bytes 9437184
  57.7 0.6 %copy.7 = f32[2,2,12,128]{3,1,2,0:T(2,128)} copy(f32[2,2,12,128]{3,1,2,0:T(2,128)S(1)} %bitcast.2) | data formatting | bytes 49152

commit v13 on v12

--- a/solution.py
+++ b/solution.py
@@ -282,14 +282,13 @@
 
     def step(u):
         wait_inputs(u)
-        compute([(0, u + 2), (1, u)])
+        compute([(0, u + 1), (1, u)])
         pl.when(u < HEADS - LAST)(lambda: start_outputs(u))
 
-    compute([(0, 0), (0, 1)])
-    each(HEADS - 2, step)
-    wait_inputs(HEADS - 2)
+    compute([(0, 0)])
+    each(HEADS - 1, step)
     wait_inputs(HEADS - 1)
-    compute([(1, HEADS - 2), (1, HEADS - 1)])
+    compute([(1, HEADS - 1)])
 
     size = 2 * HEADS // near_h
 

time: 58.4 us -> 58.2 us (level)
  no operation moved by 1% of the time
where the time goes in v13:
time: 58.2 us; the launch traced here: 58.1 us
  Pallas kernels  54.6 us (94%)
  local copies, waits for them, and re-layouts  2.8 us (5%)
  between operations  0.64 us (1%)
    pallas_call x1, Pallas kernels, shards(): pl.pallas_call(functools.partial(grad_kernel, n_t, n_h), out_shape=(pltpu...  54.6 us
    unnamed x2, local copies, waits for them, and re-layouts  2.8 us

profile of v13, /device:TPU:1, one launch (start us, length us, event | category | flops | bytes accessed | tf_op | source)
XLA Modules:
  0.0 58.1 jit_solution(5664317776016786692)
XLA Ops:
  0.6 54.6 %shard_map.41 = (bf16[2,3,2,8,16,1536]{5,4,3,2,1,0:T(8,128)(2,1)S(1)}, f32[2,12,2,128]{3,2,1,0:T(2,128)S(1)}) custom-call(bf16[2,4,2,8,16,1536]{5,4,3,2,1,0:T(8,128)(2,1)} %saved.1, f32[2,12,2,128]{3,2,1,0:T(2,128)} %bitcast.3), custom_call_target="tpu_custom_call" | custom-call | tf_op jit(solution)/shard_map/pallas_call | solution.py:351
  55.3 2.2 %copy.6 = bf16[2,3,2,8,16,1536]{5,4,3,2,1,0:T(8,128)(2,1)} copy(bf16[2,3,2,8,16,1536]{5,4,3,2,1,0:T(8,128)(2,1)S(1)} %get-tuple-element.6) | data formatting | bytes 9437184
  57.5 0.6 %copy.7 = f32[2,2,12,128]{3,1,2,0:T(2,128)} copy(f32[2,2,12,128]{3,1,2,0:T(2,128)S(1)} %bitcast.2) | data formatting | bytes 49152
